TPU v7x, 256 devices: a whole 4x4x8 slice. The times are simulated.
256 devices in a mesh: owner: 64 (over x, z, core), group: 4 (over y).
Axes of the slice: x: 4, y: 4, z: 8, core: 2. Of those that a mesh axis runs over, the one named last changes fastest.
Arguments:
- table: float32 [524288, 128], P(('owner', 'group')), may hold values from -0.6 to 0.6
- accum: float32 [524288], P(('owner', 'group')), may hold values from 0.0001 to 0.01
- requests: int32 [3, 64, 4, 64, 4], P(None, 'owner', 'group'), may hold values from 0 to 2047
- members: int32 [3, 32768, 26, 4], P(None, ('owner', 'group')), may hold values from 0 to 255
- labels: int32 [3, 32768], P(None, ('owner', 'group')), may hold values from 0 to 1
- down_proj: bfloat16 [3328, 256], replicated, may hold values from -0.109375 to 0.109375
- up_proj: bfloat16 [256, 3328], replicated, may hold values from -0.375 to 0.375
- cross_bias: float32 [3328], replicated, may hold values from -3 to 3
- out_weight: bfloat16 [3328], replicated, may hold values from -0.109375 to 0.109375
Outputs:
- table_new: float32 [524288, 128], P(('owner', 'group'))
- accum_new: float32 [524288], P(('owner', 'group'))
- grad_down: float32 [3328, 256], P(('owner', 'group'))
- grad_up: float32 [256, 3328], P(None, ('owner', 'group'))
- grad_bias: float32 [3328], P(('owner', 'group'))
- grad_out: float32 [3328], P(('owner', 'group'))
All inputs are finite; a program needn't handle non-finite values.
Results may differ from a plain program's by a relative error of at most 0.008.
Values may be sent and summed in bfloat16 or wider, within the bound.
A program may use at most 128 MiB of HBM per device.

v0:
```python
import jax
import jax.numpy as jnp
from jax import lax
from jax.sharding import PartitionSpec as P

NB = 26
BAGLEN = 4
STEPS = 3


learn_rate = 0.05


def reduce_dense(grads):
    return (
        lax.psum_scatter(grads[0], ("owner", "group"), scatter_dimension=0, tiled=True),
        lax.psum_scatter(grads[1], ("owner", "group"), scatter_dimension=1, tiled=True),
        lax.psum_scatter(grads[2], ("owner", "group"), scatter_dimension=0, tiled=True),
        lax.psum_scatter(grads[3], ("owner", "group"), scatter_dimension=0, tiled=True),
    )


def local(table, accum, requests, members, labels, down_proj, up_proj, cross_bias, out_weight):
    owners = lax.axis_size("owner")
    slots = requests.shape[4]
    fetch_rows = owners * slots
    tok_rows = members.shape[1]
    width = table.shape[1]
    d_in = down_proj.shape[0]
    row_count = table.shape[0]
    positions = jnp.arange(fetch_rows, dtype=jnp.int32)
    sums = (
        jnp.zeros((d_in, down_proj.shape[1]), jnp.float32),
        jnp.zeros(up_proj.shape, jnp.float32),
        jnp.zeros((d_in,), jnp.float32),
        jnp.zeros((d_in,), jnp.float32),
    )
    shares = None
    out_f = out_weight.astype(jnp.float32)
    for step in range(STEPS):
        current = table
        wanted = lax.all_to_all(
            requests[step, 0, 0], "owner", split_axis=0, concat_axis=0, tiled=True
        )
        rows = current[wanted].astype(jnp.bfloat16)
        returned = lax.all_to_all(rows, "owner", split_axis=0, concat_axis=0, tiled=True)
        fetched = returned
        fetched = fetched.reshape(fetch_rows, width)
        mem = members[step].reshape(tok_rows * NB, BAGLEN)
        counts_f = jnp.zeros((tok_rows * NB, fetch_rows), jnp.float32)
        for member in range(BAGLEN):
            counts_f = counts_f + (mem[:, member][:, None] == positions[None, :]).astype(
                jnp.float32
            )
        counts = counts_f.astype(jnp.bfloat16)
        pooled = jnp.dot(counts, fetched, preferred_element_type=jnp.float32)
        x0 = pooled.reshape(tok_rows, d_in).astype(jnp.bfloat16)
        low = jnp.dot(x0, down_proj, preferred_element_type=jnp.float32).astype(jnp.bfloat16)
        gate = jnp.dot(low, up_proj, preferred_element_type=jnp.float32) + cross_bias
        x0f = x0.astype(jnp.float32)
        x1 = (x0f * gate + x0f).astype(jnp.bfloat16)
        logit = jnp.dot(x1, out_weight, preferred_element_type=jnp.float32)
        dlogit = jax.nn.sigmoid(logit) - labels[step].astype(jnp.float32)
        dx1 = dlogit[:, None] * out_f[None, :]
        dgate = (dx1 * x0f).astype(jnp.bfloat16)
        dlow = lax.dot_general(
            dgate, up_proj, (((1,), (1,)), ((), ())), preferred_element_type=jnp.float32
        ).astype(jnp.bfloat16)
        dx0 = dx1 * (gate + 1.0) + lax.dot_general(
            dlow, down_proj, (((1,), (1,)), ((), ())), preferred_element_type=jnp.float32
        )
        dpooled = dx0.astype(jnp.bfloat16).reshape(tok_rows * NB, width)
        gfetch = lax.dot_general(
            counts, dpooled, (((0,), (0,)), ((), ())), preferred_element_type=jnp.float32
        )
        arrived = lax.all_to_all(
            gfetch.reshape(owners, slots, width), "owner", split_axis=0, concat_axis=0, tiled=True
        )
        row_grad = jax.ops.segment_sum(
            arrived.reshape(fetch_rows, width), wanted.reshape(fetch_rows), row_count
        )
        accum = accum + jnp.mean(row_grad * row_grad, axis=1)
        table = table - learn_rate * row_grad / jnp.sqrt(accum)[:, None]
        terms = (
            lax.dot_general(x0, dlow, (((0,), (0,)), ((), ())), preferred_element_type=jnp.float32),
            lax.dot_general(
                low, dgate, (((0,), (0,)), ((), ())), preferred_element_type=jnp.float32
            ),
            jnp.sum(dgate.astype(jnp.float32), axis=0),
            jnp.sum(x1.astype(jnp.float32) * dlogit[:, None], axis=0),
        )
        sums = tuple((a + b for a, b in zip(sums, terms)))
    shares = reduce_dense(sums)
    scale = 1.0 / (STEPS * tok_rows * owners * lax.axis_size("group"))
    return (
        table,
        accum,
        shares[0] * scale,
        shares[1] * scale,
        shares[2] * scale,
        shares[3] * scale,
    )


def solution(mesh):
    in_specs = (
        P(("owner", "group"), None),
        P(("owner", "group")),
        P(None, "owner", "group", None, None),
        P(None, ("owner", "group"), None, None),
        P(None, ("owner", "group")),
        P(),
        P(),
        P(),
        P(),
    )
    out_specs = (
        P(("owner", "group"), None),
        P(("owner", "group")),
        P(("owner", "group"), None),
        P(None, ("owner", "group")),
        P(("owner", "group")),
        P(("owner", "group")),
    )
    return jax.shard_map(local, mesh=mesh, in_specs=in_specs, out_specs=out_specs, check_vma=False)
```

profile of v0, /device:TPU:32, one launch (start us, length us, event | category | flops | bytes accessed | tf_op | source)
XLA Modules:
  0.0 1612.8 jit_solution(3369958211012779739)
XLA Ops:
  2.2 11.6 all-to-all-start.6
  22.4 6.8 all-to-all-start.3
  29.2 8.5 all-to-all-done.3
  37.7 5.4 all-to-all-start
  43.3 8.5 all-to-all-done
  53.2 6.0 all-to-all-start.1
  62.7 5.5 all-to-all-done.1
  68.2 4.8 convolution_convert_fusion.2
  88.6 6.1 all-to-all-start.2
  98.4 6.4 all-to-all-done.2
  114.3 5.8 all-to-all-start.4
  123.8 5.2 all-to-all-done.4
  128.9 6.0 convolution_convert_fusion.1
  150.4 6.1 all-to-all-start.5
  156.6 4.8 convolution_add_fusion.1
  161.3 5.1 all-to-all-done.5
  176.7 6.1 all-to-all-start.7
  182.9 4.7 convolution_add_fusion.3
  191.6 6.0 convolution_convert_fusion
  210.6 657.8 %fusion.59 = (f32[16,256]{1,0:T(8,128)}, f32[256,16]{0,1:T(8,128)S(1)}) fusion(f32[3328,256]{1,0:T(8,128)} %convolution_add_fusion.2, f32[256,3328]{0,1:T(8,128)} %convolution_add_fusion), kind=kCustom, calls=%all-reduce-scatter.2 | all-reduce-scatter fusion | flops 2097153 | bytes 6848512
  880.8 21.6 %collective-permute-start.42 = (f32[16,256]{1,0:T(8,128)}, f32[16,256]{1,0:T(8,128)S(1)}, u32[]{:S(2)}, u32[]{:S(2)}) collective-permute-start(f32[16,256]{1,0:T(8,128)} %get-tuple-element.28), channel_id=1, source_target_pairs={{0,43},{1,44},{2,45},{3,46},{4,47},{5,48},{6,49},{7,50},{8,51},{9,... | collective-permute-start | bytes 49160
  904.3 6.0 collective-permute-start.40
  911.7 19.5 %collective-permute-start.38 = (f32[16,256]{1,0:T(8,128)}, f32[16,256]{1,0:T(8,128)S(1)}, u32[]{:S(2)}, u32[]{:S(2)}) collective-permute-start(f32[16,256]{1,0:T(8,128)} %get-tuple-element.28), channel_id=1, source_target_pairs={{0,39},{1,40},{2,41},{3,42},{4,43},{5,44},{6,45},{7,46},{8,47},{9,... | collective-permute-start | bytes 49160
  931.2 4.9 collective-permute-start.37
  945.4 6.2 collective-permute-start.31
  951.7 5.2 collective-permute-start.30
  965.3 5.0 collective-permute-start.25
  974.2 4.2 collective-permute-start.22
  1001.6 5.9 collective-permute-start.12
  1007.5 13.1 collective-permute-start.11
  1020.7 13.1 collective-permute-start.10
  1033.8 13.7 collective-permute-start.9
  1047.6 13.1 collective-permute-start.8
  1060.7 12.6 collective-permute-start.7
  1073.3 13.1 collective-permute-start.6
  1086.5 13.1 collective-permute-start.5
  1099.6 13.1 collective-permute-start.4
  1112.7 13.1 collective-permute-start.3
  1125.9 13.1 collective-permute-start.2
  1139.0 13.1 collective-permute-start.1
  1152.2 13.1 collective-permute-start
  1165.3 9.5 collective-permute-start.94
  1174.8 4.5 collective-permute-start.93
  1182.8 5.4 collective-permute-start.91
  1188.2 6.4 collective-permute-start.90
  1244.6 5.3 multiply_reduce_fusion.1
  1282.8 6.6 all-to-all-start.8
  1293.5 5.5 collective-permute-start.61
  1299.1 9.1 collective-permute-start.60
  1308.2 13.1 collective-permute-start.59
  1321.3 13.1 collective-permute-start.58
  1334.5 92.4 %all-reduce.6 = (f32[3328]{0:T(1024)S(1)}, f32[3328]{0:T(1024)S(1)}) all-reduce(f32[3328]{0:T(1024)S(1)} %get-tuple-element.43, f32[3328]{0:T(1024)S(1)} %get-tuple-element.42), channel_id=4, replica_groups=mesh['owner'=64,'group'=4] {'owner','group'}, use_global_device_ids=true, to_apply=%region_11.0.clone | all-reduce | flops 6656 | bytes 53248
  1427.0 10.6 collective-permute-start.57
  1437.5 13.1 collective-permute-start.56
  1450.7 13.1 collective-permute-start.55
  1463.8 13.1 collective-permute-start.54
  1477.0 13.1 collective-permute-start.53
  1490.7 13.1 collective-permute-start.52
  1503.8 13.1 collective-permute-start.51
  1517.0 13.1 collective-permute-start.50
  1530.1 13.1 collective-permute-start.49
  1543.3 13.1 collective-permute-start.48
  1557.3 14.9 concatenate
  1573.5 33.0 %concatenate.1 = f32[256,781]{0,1:T(8,128)S(1)} concatenate(f32[256,13]{0,1:T(8,128)S(1)} %copy-done.36, f32[256,16]{0,1:T(8,128)} %collective-permute-done.94, f32[256,16]{0,1:T(8,128)} %collective-permute-done.93, f32[256,16]{0,1:T(8,128)} %collective-permute-done.92, f32[256,16]{0,1:T(8,128)} %collective-permute-done.91, f32[256,16]{0,1:T(8,128)} %collective-permute-done.90, ...), dimensions={1} | concatenate | bytes 1599488
  (514 shorter events, 247.8 us)
Async XLA Ops:
  2.2 20.1 %all-to-all-start.6 = ((s32[64,1,4]{2,1,0:T(1,128)}), s32[64,1,4]{2,1,0:T(1,128)S(1)}, u32[]{:S(2)}, u32[]{:S(2)}) async-start(s32[64,1,4]{2,1,0:T(1,128)} %bitcast.14), calls=%async_computation.6 | async-start | bytes 65536 | tf_op jit(solution)/shard_map/all_to_all | solution.py:42
  869.6 32.7 %collective-permute-start.46 = (f32[16,256]{1,0:T(8,128)}, f32[16,256]{1,0:T(8,128)S(1)}, u32[]{:S(2)}, u32[]{:S(2)}) collective-permute-start(f32[16,256]{1,0:T(8,128)} %get-tuple-element.28), channel_id=1, source_target_pairs={{0,47},{1,48},{2,49},{3,50},{4,51},{5,52},{6,53},{7,54},{8,55},{9,... | collective-permute-start | bytes 49160
  870.9 33.4 %collective-permute-start.45 = (f32[16,256]{1,0:T(8,128)}, f32[16,256]{1,0:T(8,128)S(1)}, u32[]{:S(2)}, u32[]{:S(2)}) collective-permute-start(f32[16,256]{1,0:T(8,128)} %get-tuple-element.28), channel_id=1, source_target_pairs={{0,46},{1,47},{2,48},{3,49},{4,50},{5,51},{6,52},{7,53},{8,54},{9,... | collective-permute-start | bytes 49160
  872.2 38.1 %collective-permute-start.44 = (f32[16,256]{1,0:T(8,128)}, f32[16,256]{1,0:T(8,128)S(1)}, u32[]{:S(2)}, u32[]{:S(2)}) collective-permute-start(f32[16,256]{1,0:T(8,128)} %get-tuple-element.28), channel_id=1, source_target_pairs={{0,45},{1,46},{2,47},{3,48},{4,49},{5,50},{6,51},{7,52},{8,53},{9,... | collective-permute-start | bytes 49160
  873.5 38.1 %collective-permute-start.43 = (f32[16,256]{1,0:T(8,128)}, f32[16,256]{1,0:T(8,128)S(1)}, u32[]{:S(2)}, u32[]{:S(2)}) collective-permute-start(f32[16,256]{1,0:T(8,128)} %get-tuple-element.28), channel_id=1, source_target_pairs={{0,44},{1,45},{2,46},{3,47},{4,48},{5,49},{6,50},{7,51},{8,52},{9,... | collective-permute-start | bytes 49160
  880.8 50.4 %collective-permute-start.42 = (f32[16,256]{1,0:T(8,128)}, f32[16,256]{1,0:T(8,128)S(1)}, u32[]{:S(2)}, u32[]{:S(2)}) collective-permute-start(f32[16,256]{1,0:T(8,128)} %get-tuple-element.28), channel_id=1, source_target_pairs={{0,43},{1,44},{2,45},{3,46},{4,47},{5,48},{6,49},{7,50},{8,51},{9,... | collective-permute-start | bytes 49160
  902.4 33.7 %collective-permute-start.41 = (f32[16,256]{1,0:T(8,128)}, f32[16,256]{1,0:T(8,128)S(1)}, u32[]{:S(2)}, u32[]{:S(2)}) collective-permute-start(f32[16,256]{1,0:T(8,128)} %get-tuple-element.28), channel_id=1, source_target_pairs={{0,42},{1,43},{2,44},{3,45},{4,46},{5,47},{6,48},{7,49},{8,50},{9,... | collective-permute-start | bytes 49160
  904.3 33.1 %collective-permute-start.40 = (f32[16,256]{1,0:T(8,128)}, f32[16,256]{1,0:T(8,128)S(1)}, u32[]{:S(2)}, u32[]{:S(2)}) collective-permute-start(f32[16,256]{1,0:T(8,128)} %get-tuple-element.28), channel_id=1, source_target_pairs={{0,41},{1,42},{2,43},{3,44},{4,45},{5,46},{6,47},{7,48},{8,49},{9,... | collective-permute-start | bytes 49160
  910.3 28.8 %collective-permute-start.39 = (f32[16,256]{1,0:T(8,128)}, f32[16,256]{1,0:T(8,128)S(1)}, u32[]{:S(2)}, u32[]{:S(2)}) collective-permute-start(f32[16,256]{1,0:T(8,128)} %get-tuple-element.28), channel_id=1, source_target_pairs={{0,40},{1,41},{2,42},{3,43},{4,44},{5,45},{6,46},{7,47},{8,48},{9,... | collective-permute-start | bytes 49160
  911.7 30.3 %collective-permute-start.38 = (f32[16,256]{1,0:T(8,128)}, f32[16,256]{1,0:T(8,128)S(1)}, u32[]{:S(2)}, u32[]{:S(2)}) collective-permute-start(f32[16,256]{1,0:T(8,128)} %get-tuple-element.28), channel_id=1, source_target_pairs={{0,39},{1,40},{2,41},{3,42},{4,43},{5,44},{6,45},{7,46},{8,47},{9,... | collective-permute-start | bytes 49160
  939.1 17.8 %collective-permute-start.34 = (f32[16,256]{1,0:T(8,128)}, f32[16,256]{1,0:T(8,128)S(1)}, u32[]{:S(2)}, u32[]{:S(2)}) collective-permute-start(f32[16,256]{1,0:T(8,128)} %get-tuple-element.28), channel_id=1, source_target_pairs={{0,35},{1,36},{2,37},{3,38},{4,39},{5,40},{6,41},{7,42},{8,43},{9,... | collective-permute-start | bytes 49160
  943.7 16.8 %collective-permute-start.32 = (f32[16,256]{1,0:T(8,128)}, f32[16,256]{1,0:T(8,128)S(1)}, u32[]{:S(2)}, u32[]{:S(2)}) collective-permute-start(f32[16,256]{1,0:T(8,128)} %get-tuple-element.28), channel_id=1, source_target_pairs={{0,33},{1,34},{2,35},{3,36},{4,37},{5,38},{6,39},{7,40},{8,41},{9,... | collective-permute-start | bytes 49160
  945.4 16.8 %collective-permute-start.31 = (f32[16,256]{1,0:T(8,128)}, f32[16,256]{1,0:T(8,128)S(1)}, u32[]{:S(2)}, u32[]{:S(2)}) collective-permute-start(f32[16,256]{1,0:T(8,128)} %get-tuple-element.28), channel_id=1, source_target_pairs={{0,32},{1,33},{2,34},{3,35},{4,36},{5,37},{6,38},{7,39},{8,40},{9,... | collective-permute-start | bytes 49160
  993.6 27.1 %collective-permute-start.15 = (f32[16,256]{1,0:T(8,128)}, f32[16,256]{1,0:T(8,128)S(1)}, u32[]{:S(2)}, u32[]{:S(2)}) collective-permute-start(f32[16,256]{1,0:T(8,128)} %get-tuple-element.28), channel_id=1, source_target_pairs={{0,16},{1,17},{2,18},{3,19},{4,20},{5,21},{6,22},{7,23},{8,24},{9,... | collective-permute-start | bytes 49160
  995.7 38.1 %collective-permute-start.14 = (f32[16,256]{1,0:T(8,128)}, f32[16,256]{1,0:T(8,128)S(1)}, u32[]{:S(2)}, u32[]{:S(2)}) collective-permute-start(f32[16,256]{1,0:T(8,128)} %get-tuple-element.28), channel_id=1, source_target_pairs={{0,15},{1,16},{2,17},{3,18},{4,19},{5,20},{6,21},{7,22},{8,23},{9,... | collective-permute-start | bytes 49160
  999.5 48.1 %collective-permute-start.13 = (f32[16,256]{1,0:T(8,128)}, f32[16,256]{1,0:T(8,128)S(1)}, u32[]{:S(2)}, u32[]{:S(2)}) collective-permute-start(f32[16,256]{1,0:T(8,128)} %get-tuple-element.28), channel_id=1, source_target_pairs={{0,14},{1,15},{2,16},{3,17},{4,18},{5,19},{6,20},{7,21},{8,22},{9,... | collective-permute-start | bytes 49160
  1001.6 59.1 %collective-permute-start.12 = (f32[16,256]{1,0:T(8,128)}, f32[16,256]{1,0:T(8,128)S(1)}, u32[]{:S(2)}, u32[]{:S(2)}) collective-permute-start(f32[16,256]{1,0:T(8,128)} %get-tuple-element.28), channel_id=1, source_target_pairs={{0,13},{1,14},{2,15},{3,16},{4,17},{5,18},{6,19},{7,20},{8,21},{9,... | collective-permute-start | bytes 49160
  1007.5 65.7 %collective-permute-start.11 = (f32[16,256]{1,0:T(8,128)}, f32[16,256]{1,0:T(8,128)S(1)}, u32[]{:S(2)}, u32[]{:S(2)}) collective-permute-start(f32[16,256]{1,0:T(8,128)} %get-tuple-element.28), channel_id=1, source_target_pairs={{0,12},{1,13},{2,14},{3,15},{4,16},{5,17},{6,18},{7,19},{8,20},{9,... | collective-permute-start | bytes 49160
  1020.7 65.7 %collective-permute-start.10 = (f32[16,256]{1,0:T(8,128)}, f32[16,256]{1,0:T(8,128)S(1)}, u32[]{:S(2)}, u32[]{:S(2)}) collective-permute-start(f32[16,256]{1,0:T(8,128)} %get-tuple-element.28), channel_id=1, source_target_pairs={{0,11},{1,12},{2,13},{3,14},{4,15},{5,16},{6,17},{7,18},{8,19},{9,... | collective-permute-start | bytes 49160
  1033.8 65.7 %collective-permute-start.9 = (f32[16,256]{1,0:T(8,128)}, f32[16,256]{1,0:T(8,128)}, u32[]{:S(2)}, u32[]{:S(2)}) collective-permute-start(f32[16,256]{1,0:T(8,128)} %get-tuple-element.28), channel_id=1, source_target_pairs={{0,10},{1,11},{2,12},{3,13},{4,14},{5,15},{6,16},{7,17},{8,18},{9,... | collective-permute-start | bytes 49160
  1047.6 65.2 %collective-permute-start.8 = (f32[16,256]{1,0:T(8,128)}, f32[16,256]{1,0:T(8,128)}, u32[]{:S(2)}, u32[]{:S(2)}) collective-permute-start(f32[16,256]{1,0:T(8,128)} %get-tuple-element.28), channel_id=1, source_target_pairs={{0,9},{1,10},{2,11},{3,12},{4,13},{5,14},{6,15},{7,16},{8,17},{9,1... | collective-permute-start | bytes 49160
  1060.7 65.1 %collective-permute-start.7 = (f32[16,256]{1,0:T(8,128)}, f32[16,256]{1,0:T(8,128)}, u32[]{:S(2)}, u32[]{:S(2)}) collective-permute-start(f32[16,256]{1,0:T(8,128)} %get-tuple-element.28), channel_id=1, source_target_pairs={{0,8},{1,9},{2,10},{3,11},{4,12},{5,13},{6,14},{7,15},{8,16},{9,17... | collective-permute-start | bytes 49160
  1073.3 65.7 %collective-permute-start.6 = (f32[16,256]{1,0:T(8,128)}, f32[16,256]{1,0:T(8,128)}, u32[]{:S(2)}, u32[]{:S(2)}) collective-permute-start(f32[16,256]{1,0:T(8,128)} %get-tuple-element.28), channel_id=1, source_target_pairs={{0,7},{1,8},{2,9},{3,10},{4,11},{5,12},{6,13},{7,14},{8,15},{9,16}... | collective-permute-start | bytes 49160
  1086.5 65.7 %collective-permute-start.5 = (f32[16,256]{1,0:T(8,128)}, f32[16,256]{1,0:T(8,128)}, u32[]{:S(2)}, u32[]{:S(2)}) collective-permute-start(f32[16,256]{1,0:T(8,128)} %get-tuple-element.28), channel_id=1, source_target_pairs={{0,6},{1,7},{2,8},{3,9},{4,10},{5,11},{6,12},{7,13},{8,14},{9,15},... | collective-permute-start | bytes 49160
  1099.6 65.7 %collective-permute-start.4 = (f32[16,256]{1,0:T(8,128)}, f32[16,256]{1,0:T(8,128)}, u32[]{:S(2)}, u32[]{:S(2)}) collective-permute-start(f32[16,256]{1,0:T(8,128)} %get-tuple-element.28), channel_id=1, source_target_pairs={{0,5},{1,6},{2,7},{3,8},{4,9},{5,10},{6,11},{7,12},{8,13},{9,14},{... | collective-permute-start | bytes 49160
  1112.7 62.1 %collective-permute-start.3 = (f32[16,256]{1,0:T(8,128)}, f32[16,256]{1,0:T(8,128)}, u32[]{:S(2)}, u32[]{:S(2)}) collective-permute-start(f32[16,256]{1,0:T(8,128)} %get-tuple-element.28), channel_id=1, source_target_pairs={{0,4},{1,5},{2,6},{3,7},{4,8},{5,9},{6,10},{7,11},{8,12},{9,13},{1... | collective-permute-start | bytes 49160
  1125.9 53.5 %collective-permute-start.2 = (f32[16,256]{1,0:T(8,128)}, f32[16,256]{1,0:T(8,128)}, u32[]{:S(2)}, u32[]{:S(2)}) collective-permute-start(f32[16,256]{1,0:T(8,128)} %get-tuple-element.28), channel_id=1, source_target_pairs={{0,3},{1,4},{2,5},{3,6},{4,7},{5,8},{6,9},{7,10},{8,11},{9,12},{10... | collective-permute-start | bytes 49160
  1139.0 43.8 %collective-permute-start.1 = (f32[16,256]{1,0:T(8,128)}, f32[16,256]{1,0:T(8,128)}, u32[]{:S(2)}, u32[]{:S(2)}) collective-permute-start(f32[16,256]{1,0:T(8,128)} %get-tuple-element.28), channel_id=1, source_target_pairs={{0,2},{1,3},{2,4},{3,5},{4,6},{5,7},{6,8},{7,9},{8,10},{9,11},{10,... | collective-permute-start | bytes 49160
  1152.2 36.1 %collective-permute-start = (f32[16,256]{1,0:T(8,128)}, f32[16,256]{1,0:T(8,128)}, u32[]{:S(2)}, u32[]{:S(2)}) collective-permute-start(f32[16,256]{1,0:T(8,128)} %get-tuple-element.28), channel_id=1, source_target_pairs={{0,1},{1,2},{2,3},{3,4},{4,5},{5,6},{6,7},{7,8},{8,9},{9,10},{10,1... | collective-permute-start | bytes 49160
  1165.3 29.3 %collective-permute-start.94 = (f32[256,16]{0,1:T(8,128)S(1)}, f32[256,16]{0,1:T(8,128)}, u32[]{:S(2)}, u32[]{:S(2)}) collective-permute-start(f32[256,16]{0,1:T(8,128)S(1)} %get-tuple-element.29), channel_id=1, source_target_pairs={{0,47},{1,48},{2,49},{3,50},{4,51},{5,52},{6,53},{7,54},{8,55},{9,... | collective-permute-start | bytes 49160
  1174.8 23.4 %collective-permute-start.93 = (f32[256,16]{0,1:T(8,128)S(1)}, f32[256,16]{0,1:T(8,128)}, u32[]{:S(2)}, u32[]{:S(2)}) collective-permute-start(f32[256,16]{0,1:T(8,128)S(1)} %get-tuple-element.29), channel_id=1, source_target_pairs={{0,46},{1,47},{2,48},{3,49},{4,50},{5,51},{6,52},{7,53},{8,54},{9,... | collective-permute-start | bytes 49160
  1179.3 20.8 %collective-permute-start.92 = (f32[256,16]{0,1:T(8,128)S(1)}, f32[256,16]{0,1:T(8,128)}, u32[]{:S(2)}, u32[]{:S(2)}) collective-permute-start(f32[256,16]{0,1:T(8,128)S(1)} %get-tuple-element.29), channel_id=1, source_target_pairs={{0,45},{1,46},{2,47},{3,48},{4,49},{5,50},{6,51},{7,52},{8,53},{9,... | collective-permute-start | bytes 49160
  1182.8 19.2 %collective-permute-start.91 = (f32[256,16]{0,1:T(8,128)S(1)}, f32[256,16]{0,1:T(8,128)}, u32[]{:S(2)}, u32[]{:S(2)}) collective-permute-start(f32[256,16]{0,1:T(8,128)S(1)} %get-tuple-element.29), channel_id=1, source_target_pairs={{0,44},{1,45},{2,46},{3,47},{4,48},{5,49},{6,50},{7,51},{8,52},{9,... | collective-permute-start | bytes 49160
  1213.6 17.7 %collective-permute-start.82 = (f32[256,16]{0,1:T(8,128)S(1)}, f32[256,16]{0,1:T(8,128)}, u32[]{:S(2)}, u32[]{:S(2)}) collective-permute-start(f32[256,16]{0,1:T(8,128)S(1)} %get-tuple-element.29), channel_id=1, source_target_pairs={{0,35},{1,36},{2,37},{3,38},{4,39},{5,40},{6,41},{7,42},{8,43},{9,... | collective-permute-start | bytes 49160
  1219.4 17.2 %collective-permute-start.80 = (f32[256,16]{0,1:T(8,128)S(1)}, f32[256,16]{0,1:T(8,128)}, u32[]{:S(2)}, u32[]{:S(2)}) collective-permute-start(f32[256,16]{0,1:T(8,128)S(1)} %get-tuple-element.29), channel_id=1, source_target_pairs={{0,33},{1,34},{2,35},{3,36},{4,37},{5,38},{6,39},{7,40},{8,41},{9,... | collective-permute-start | bytes 49160
  1225.0 16.9 %collective-permute-start.78 = (f32[256,16]{0,1:T(8,128)S(1)}, f32[256,16]{0,1:T(8,128)}, u32[]{:S(2)}, u32[]{:S(2)}) collective-permute-start(f32[256,16]{0,1:T(8,128)S(1)} %get-tuple-element.29), channel_id=1, source_target_pairs={{0,31},{1,32},{2,33},{3,34},{4,35},{5,36},{6,37},{7,38},{8,39},{9,... | collective-permute-start | bytes 49160
  1231.3 18.7 %collective-permute-start.77 = (f32[256,16]{0,1:T(8,128)S(1)}, f32[256,16]{0,1:T(8,128)S(1)}, u32[]{:S(2)}, u32[]{:S(2)}) collective-permute-start(f32[256,16]{0,1:T(8,128)S(1)} %get-tuple-element.29), channel_id=1, source_target_pairs={{0,30},{1,31},{2,32},{3,33},{4,34},{5,35},{6,36},{7,37},{8,38},{9,... | collective-permute-start | bytes 49160
  1234.0 19.8 %collective-permute-start.76 = (f32[256,16]{0,1:T(8,128)S(1)}, f32[256,16]{0,1:T(8,128)S(1)}, u32[]{:S(2)}, u32[]{:S(2)}) collective-permute-start(f32[256,16]{0,1:T(8,128)S(1)} %get-tuple-element.29), channel_id=1, source_target_pairs={{0,29},{1,30},{2,31},{3,32},{4,33},{5,34},{6,35},{7,36},{8,37},{9,... | collective-permute-start | bytes 49160
  1236.6 19.2 %collective-permute-start.75 = (f32[256,16]{0,1:T(8,128)S(1)}, f32[256,16]{0,1:T(8,128)S(1)}, u32[]{:S(2)}, u32[]{:S(2)}) collective-permute-start(f32[256,16]{0,1:T(8,128)S(1)} %get-tuple-element.29), channel_id=1, source_target_pairs={{0,28},{1,29},{2,30},{3,31},{4,32},{5,33},{6,34},{7,35},{8,36},{9,... | collective-permute-start | bytes 49160
  1238.2 21.0 %collective-permute-start.74 = (f32[256,16]{0,1:T(8,128)S(1)}, f32[256,16]{0,1:T(8,128)S(1)}, u32[]{:S(2)}, u32[]{:S(2)}) collective-permute-start(f32[256,16]{0,1:T(8,128)S(1)} %get-tuple-element.29), channel_id=1, source_target_pairs={{0,27},{1,28},{2,29},{3,30},{4,31},{5,32},{6,33},{7,34},{8,35},{9,... | collective-permute-start | bytes 49160
  1242.0 19.5 %collective-permute-start.73 = (f32[256,16]{0,1:T(8,128)S(1)}, f32[256,16]{0,1:T(8,128)S(1)}, u32[]{:S(2)}, u32[]{:S(2)}) collective-permute-start(f32[256,16]{0,1:T(8,128)S(1)} %get-tuple-element.29), channel_id=1, source_target_pairs={{0,26},{1,27},{2,28},{3,29},{4,30},{5,31},{6,32},{7,33},{8,34},{9,... | collective-permute-start | bytes 49160
  1249.9 17.7 %collective-permute-start.72 = (f32[256,16]{0,1:T(8,128)S(1)}, f32[256,16]{0,1:T(8,128)}, u32[]{:S(2)}, u32[]{:S(2)}) collective-permute-start(f32[256,16]{0,1:T(8,128)S(1)} %get-tuple-element.29), channel_id=1, source_target_pairs={{0,25},{1,26},{2,27},{3,28},{4,29},{5,30},{6,31},{7,32},{8,33},{9,... | collective-permute-start | bytes 49160
  1255.8 17.3 %collective-permute-start.70 = (f32[256,16]{0,1:T(8,128)S(1)}, f32[256,16]{0,1:T(8,128)}, u32[]{:S(2)}, u32[]{:S(2)}) collective-permute-start(f32[256,16]{0,1:T(8,128)S(1)} %get-tuple-element.29), channel_id=1, source_target_pairs={{0,23},{1,24},{2,25},{3,26},{4,27},{5,28},{6,29},{7,30},{8,31},{9,... | collective-permute-start | bytes 49160
  1267.6 21.8 %collective-permute-start.67 = (f32[256,16]{0,1:T(8,128)S(1)}, f32[256,16]{0,1:T(8,128)S(1)}, u32[]{:S(2)}, u32[]{:S(2)}) collective-permute-start(f32[256,16]{0,1:T(8,128)S(1)} %get-tuple-element.29), channel_id=1, source_target_pairs={{0,20},{1,21},{2,22},{3,23},{4,24},{5,25},{6,26},{7,27},{8,28},{9,... | collective-permute-start | bytes 49160
  1269.1 24.4 %collective-permute-start.66 = (f32[256,16]{0,1:T(8,128)S(1)}, f32[256,16]{0,1:T(8,128)S(1)}, u32[]{:S(2)}, u32[]{:S(2)}) collective-permute-start(f32[256,16]{0,1:T(8,128)S(1)} %get-tuple-element.29), channel_id=1, source_target_pairs={{0,19},{1,20},{2,21},{3,22},{4,23},{5,24},{6,25},{7,26},{8,27},{9,... | collective-permute-start | bytes 49160
  1273.1 25.9 %collective-permute-start.65 = (f32[256,16]{0,1:T(8,128)S(1)}, f32[256,16]{0,1:T(8,128)S(1)}, u32[]{:S(2)}, u32[]{:S(2)}) collective-permute-start(f32[256,16]{0,1:T(8,128)S(1)} %get-tuple-element.29), channel_id=1, source_target_pairs={{0,18},{1,19},{2,20},{3,21},{4,22},{5,23},{6,24},{7,25},{8,26},{9,... | collective-permute-start | bytes 49160
  1275.4 32.8 %collective-permute-start.64 = (f32[256,16]{0,1:T(8,128)S(1)}, f32[256,16]{0,1:T(8,128)S(1)}, u32[]{:S(2)}, u32[]{:S(2)}) collective-permute-start(f32[256,16]{0,1:T(8,128)S(1)} %get-tuple-element.29), channel_id=1, source_target_pairs={{0,17},{1,18},{2,19},{3,20},{4,21},{5,22},{6,23},{7,24},{8,25},{9,... | collective-permute-start | bytes 49160
  1277.3 44.0 %collective-permute-start.63 = (f32[256,16]{0,1:T(8,128)S(1)}, f32[256,16]{0,1:T(8,128)S(1)}, u32[]{:S(2)}, u32[]{:S(2)}) collective-permute-start(f32[256,16]{0,1:T(8,128)S(1)} %get-tuple-element.29), channel_id=1, source_target_pairs={{0,16},{1,17},{2,18},{3,19},{4,20},{5,21},{6,22},{7,23},{8,24},{9,... | collective-permute-start | bytes 49160
  1282.8 324.9 %all-to-all-start.8 = ((f32[64,4,128]{2,1,0:T(4,128)}), f32[64,4,128]{2,1,0:T(4,128)}, u32[]{:S(2)}, u32[]{:S(2)}) async-start(f32[64,4,128]{2,1,0:T(4,128)} %copy.35), calls=%async_computation.8 | async-start | bytes 262144 | tf_op jit(solution)/shard_map/all_to_all | solution.py:76
  1289.4 137.5 %collective-permute-start.62 = (f32[256,16]{0,1:T(8,128)S(1)}, f32[256,16]{0,1:T(8,128)S(1)}, u32[]{:S(2)}, u32[]{:S(2)}) collective-permute-start(f32[256,16]{0,1:T(8,128)S(1)} %get-tuple-element.29), channel_id=1, source_target_pairs={{0,15},{1,16},{2,17},{3,18},{4,19},{5,20},{6,21},{7,22},{8,23},{9,... | collective-permute-start | bytes 49160
  1293.5 144.0 %collective-permute-start.61 = (f32[256,16]{0,1:T(8,128)S(1)}, f32[256,16]{0,1:T(8,128)S(1)}, u32[]{:S(2)}, u32[]{:S(2)}) collective-permute-start(f32[256,16]{0,1:T(8,128)S(1)} %get-tuple-element.29), channel_id=1, source_target_pairs={{0,14},{1,15},{2,16},{3,17},{4,18},{5,19},{6,20},{7,21},{8,22},{9,... | collective-permute-start | bytes 49160
  1299.1 151.6 %collective-permute-start.60 = (f32[256,16]{0,1:T(8,128)S(1)}, f32[256,16]{0,1:T(8,128)S(1)}, u32[]{:S(2)}, u32[]{:S(2)}) collective-permute-start(f32[256,16]{0,1:T(8,128)S(1)} %get-tuple-element.29), channel_id=1, source_target_pairs={{0,13},{1,14},{2,15},{3,16},{4,17},{5,18},{6,19},{7,20},{8,21},{9,... | collective-permute-start | bytes 49160
  1308.2 155.7 %collective-permute-start.59 = (f32[256,16]{0,1:T(8,128)S(1)}, f32[256,16]{0,1:T(8,128)S(1)}, u32[]{:S(2)}, u32[]{:S(2)}) collective-permute-start(f32[256,16]{0,1:T(8,128)S(1)} %get-tuple-element.29), channel_id=1, source_target_pairs={{0,12},{1,13},{2,14},{3,15},{4,16},{5,17},{6,18},{7,19},{8,20},{9,... | collective-permute-start | bytes 49160
  1321.3 155.7 %collective-permute-start.58 = (f32[256,16]{0,1:T(8,128)S(1)}, f32[256,16]{0,1:T(8,128)S(1)}, u32[]{:S(2)}, u32[]{:S(2)}) collective-permute-start(f32[256,16]{0,1:T(8,128)S(1)} %get-tuple-element.29), channel_id=1, source_target_pairs={{0,11},{1,12},{2,13},{3,14},{4,15},{5,16},{6,17},{7,18},{8,19},{9,... | collective-permute-start | bytes 49160
  1427.0 63.8 %collective-permute-start.57 = (f32[256,16]{0,1:T(8,128)S(1)}, f32[256,16]{0,1:T(8,128)S(1)}, u32[]{:S(2)}, u32[]{:S(2)}) collective-permute-start(f32[256,16]{0,1:T(8,128)S(1)} %get-tuple-element.29), channel_id=1, source_target_pairs={{0,10},{1,11},{2,12},{3,13},{4,14},{5,15},{6,16},{7,17},{8,18},{9,... | collective-permute-start | bytes 49160
  1437.5 66.3 %collective-permute-start.56 = (f32[256,16]{0,1:T(8,128)S(1)}, f32[256,16]{0,1:T(8,128)S(1)}, u32[]{:S(2)}, u32[]{:S(2)}) collective-permute-start(f32[256,16]{0,1:T(8,128)S(1)} %get-tuple-element.29), channel_id=1, source_target_pairs={{0,9},{1,10},{2,11},{3,12},{4,13},{5,14},{6,15},{7,16},{8,17},{9,1... | collective-permute-start | bytes 49160
  1450.7 66.3 %collective-permute-start.55 = (f32[256,16]{0,1:T(8,128)S(1)}, f32[256,16]{0,1:T(8,128)S(1)}, u32[]{:S(2)}, u32[]{:S(2)}) collective-permute-start(f32[256,16]{0,1:T(8,128)S(1)} %get-tuple-element.29), channel_id=1, source_target_pairs={{0,8},{1,9},{2,10},{3,11},{4,12},{5,13},{6,14},{7,15},{8,16},{9,17... | collective-permute-start | bytes 49160
  1463.8 66.3 %collective-permute-start.54 = (f32[256,16]{0,1:T(8,128)S(1)}, f32[256,16]{0,1:T(8,128)S(1)}, u32[]{:S(2)}, u32[]{:S(2)}) collective-permute-start(f32[256,16]{0,1:T(8,128)S(1)} %get-tuple-element.29), channel_id=1, source_target_pairs={{0,7},{1,8},{2,9},{3,10},{4,11},{5,12},{6,13},{7,14},{8,15},{9,16}... | collective-permute-start | bytes 49160
  1477.0 66.3 %collective-permute-start.53 = (f32[256,16]{0,1:T(8,128)S(1)}, f32[256,16]{0,1:T(8,128)S(1)}, u32[]{:S(2)}, u32[]{:S(2)}) collective-permute-start(f32[256,16]{0,1:T(8,128)S(1)} %get-tuple-element.29), channel_id=1, source_target_pairs={{0,6},{1,7},{2,8},{3,9},{4,10},{5,11},{6,12},{7,13},{8,14},{9,15},... | collective-permute-start | bytes 49160
  1490.7 81.5 %collective-permute-start.52 = (f32[256,16]{0,1:T(8,128)S(1)}, f32[256,16]{0,1:T(8,128)S(1)}, u32[]{:S(2)}, u32[]{:S(2)}) collective-permute-start(f32[256,16]{0,1:T(8,128)S(1)} %get-tuple-element.29), channel_id=1, source_target_pairs={{0,5},{1,6},{2,7},{3,8},{4,9},{5,10},{6,11},{7,12},{8,13},{9,14},{... | collective-permute-start | bytes 49160
  1503.8 68.4 %collective-permute-start.51 = (f32[256,16]{0,1:T(8,128)S(1)}, f32[256,16]{0,1:T(8,128)S(1)}, u32[]{:S(2)}, u32[]{:S(2)}) collective-permute-start(f32[256,16]{0,1:T(8,128)S(1)} %get-tuple-element.29), channel_id=1, source_target_pairs={{0,4},{1,5},{2,6},{3,7},{4,8},{5,9},{6,10},{7,11},{8,12},{9,13},{1... | collective-permute-start | bytes 49160
  1517.0 55.3 %collective-permute-start.50 = (f32[256,16]{0,1:T(8,128)S(1)}, f32[256,16]{0,1:T(8,128)S(1)}, u32[]{:S(2)}, u32[]{:S(2)}) collective-permute-start(f32[256,16]{0,1:T(8,128)S(1)} %get-tuple-element.29), channel_id=1, source_target_pairs={{0,3},{1,4},{2,5},{3,6},{4,7},{5,8},{6,9},{7,10},{8,11},{9,12},{10... | collective-permute-start | bytes 49160
  1530.1 42.2 %collective-permute-start.49 = (f32[256,16]{0,1:T(8,128)S(1)}, f32[256,16]{0,1:T(8,128)S(1)}, u32[]{:S(2)}, u32[]{:S(2)}) collective-permute-start(f32[256,16]{0,1:T(8,128)S(1)} %get-tuple-element.29), channel_id=1, source_target_pairs={{0,2},{1,3},{2,4},{3,5},{4,6},{5,7},{6,8},{7,9},{8,10},{9,11},{10,... | collective-permute-start | bytes 49160
  1543.3 30.2 %collective-permute-start.48 = (f32[256,16]{0,1:T(8,128)S(1)}, f32[256,16]{0,1:T(8,128)}, u32[]{:S(2)}, u32[]{:S(2)}) collective-permute-start(f32[256,16]{0,1:T(8,128)S(1)} %get-tuple-element.29), channel_id=1, source_target_pairs={{0,1},{1,2},{2,3},{3,4},{4,5},{5,6},{6,7},{7,8},{8,9},{9,10},{10,1... | collective-permute-start | bytes 49160
  (177 other events, 23952.2 us)
where the time goes:
time: 1630 us; the launch traced here: 1610 us
  blocking collectives  750 us (46%)
  starting transfers between devices  630 us (39%)
  local copies, waits for them, and re-layouts  90.6 us (6%)
  matrix products  60.6 us (4%)
  waiting for transfers between devices  48.4 us (3%)
  other arithmetic  28.9 us (2%)
    unnamed x2, blocking collectives  750 us
    unnamed x96, starting transfers between devices  569 us
    unnamed x280, local copies, waits for them, and re-layouts  58.1 us
  transfers between devices with their start and end apart: 105, of which 9 were waited for; matrix products, arithmetic and copies ran while one was open for 6% of the time, Pallas kernels for 0%

commit v1 on v0

v1 whole, which is shorter than its diff:
```python
import functools

import jax
import jax.numpy as jnp
from jax import lax
from jax.experimental import pallas as pl
from jax.experimental.pallas import tpu as pltpu
from jax.sharding import PartitionSpec as P

NX, NY, NZ, NC = 4, 4, 8, 2
NXC = NX * NC
NB = 26
BAGLEN = 4
STEPS = 3
E = 128
TOK = 128
RANK = 256
D_IN = NB * E
ROWS = 2048
SLOTS = 4
FETCH = NZ * NXC * SLOTS
SLAB = 32
CH = 256
NCH = D_IN // CH
XROWS = D_IN // NX
HALF = XROWS // NC
PART = HALF // 2
BLOCK = XROWS // NZ
SHARE = 13
WIN = 24

learn_rate = 0.05
F32 = jnp.float32
BF16 = jnp.bfloat16


def nn(a, b):
    return jnp.dot(a, b, preferred_element_type=F32)


def nt(a, b):
    return lax.dot_general(a, b, (((1,), (1,)), ((), ())), preferred_element_type=F32)


def iota(shape, dim):
    return lax.broadcasted_iota(jnp.int32, shape, dim)


def onehot(mask):
    return jnp.where(mask, 1.0, 0.0).astype(BF16)


def al(value, step):
    return pl.multiple_of(value, step)


def remote(src, dst, send, recv, dev):
    copy = pltpu.make_async_remote_copy(
        src_ref=src, dst_ref=dst, send_sem=send, recv_sem=recv,
        device_id=dev, device_id_type=pl.DeviceIdType.MESH,
    )
    copy.start()
    return copy


def wait_all(copies):
    for copy in copies:
        copy.wait()


def kernel(
    table_in, accum_in, reqs, mem, labels, down, up, bias, outw,
    table, accum_out, gdu_out, bo_out,
    rq, wcol, wrow, s1, r1, s2, r2, g0, g1, g2, g3,
    down_t, up_t, bias_b, out_b, acc_b, posq,
    counts, x0s, dgs, lows, dlows, gates, x1s, bo3,
    gs, rc, ss, rx1, ry1, rx2, ry2, aa, bb, ff, rz, tt, fw,
    bo, boc, box, boy, boz,
    q1s, q1r, q2s, q2r, f1s, f1r, f2s, f2r, b1s, b1r, b2s, b2r,
    cs, cr, xs, xr, ys, yr, x2s, x2r, y2s, y2r, zs, zr, fs, fr,
    bcs, bcr, bxs, bxr, bys, byr, bzs, bzr,
):
    owner = lax.axis_index("owner")
    y = lax.axis_index("group")
    c = owner % NC
    z = (owner // NC) % NZ
    x = owner // (NC * NZ)
    xc = x * NC + c

    def dev(px, pz, pc, py):
        return ((px * NZ + pz) * NC + pc, py)

    def zpeer(k):
        pz = (z + k) % NZ
        return pz, dev(x, pz, c, y)

    def xcpeer(k):
        pxc = (xc + k) % NXC
        return pxc, dev(pxc // NC, z, pxc % NC, y)

    def xpeer(k):
        px = (x + k) % NX
        return px, dev(px, z, c, y)

    def ypeer(k):
        py = (y + k) % NY
        return py, dev(x, z, c, py)

    partner = dev(x, z, 1 - c, y)

    barrier = pltpu.get_barrier_semaphore()
    greet = [zpeer(k)[1] for k in range(1, NZ)] + [xcpeer(k)[1] for k in range(1, NXC)]
    greet += [ypeer(k)[1] for k in range(1, NY)]
    greet += [dev(x, z, 1 - c, (y + k) % NY) for k in range(1, NY)]
    for peer in greet:
        pl.semaphore_signal(barrier, inc=1, device_id=peer, device_id_type=pl.DeviceIdType.MESH)
    pl.semaphore_wait(barrier, len(greet))

    rq[xc, z] = reqs[...]
    copies = []
    for k in range(1, NZ):
        copies.append(remote(rq.at[xc, z], rq.at[xc, z], q1s.at[k], q1r.at[k], zpeer(k)[1]))

    eye = onehot(iota((CH, CH), 0) == iota((CH, CH), 1))

    def weights(i, carry):
        at = al(i * CH, CH)
        down_t[:, pl.ds(at, CH)] = nt(eye, down[pl.ds(at, CH), :]).astype(BF16)
        up_t[pl.ds(at, CH), :] = nt(eye, up[:, pl.ds(at, CH)]).astype(BF16)
        return carry

    wait_all(copies)
    copies = []
    for k in range(1, NXC):
        copies.append(remote(rq.at[xc], rq.at[xc], q2s.at[k], q2r.at[k], xcpeer(k)[1]))
    lax.fori_loop(0, NCH, weights, 0)

    def columns(i, carry):
        at = al(i * E, E)
        bias_b[pl.ds(at, E), :] = jnp.broadcast_to(bias[pl.ds(i, 1), :], (E, E)).T
        out_b[pl.ds(at, E), :] = jnp.broadcast_to(outw[pl.ds(i, 1), :], (E, E)).T
        return carry

    lax.fori_loop(0, NB, columns, 0)

    def acc_columns(i, carry):
        at = al(i * E, E)
        acc_b[pl.ds(at, E), :] = jnp.broadcast_to(accum_in[pl.ds(i, 1), :], (E, E)).T
        return carry

    lax.fori_loop(0, ROWS // E, acc_columns, 0)
    table[...] = table_in[...]
    bo3[...] = jnp.zeros_like(bo3)

    qi = iota((FETCH, E), 0)
    qb = qi // SLOTS
    q_xc = qb // NZ
    q_z = qb % NZ
    posq[...] = (((q_xc // NC) * NZ + q_z) * NC + q_xc % NC) * SLOTS + qi % SLOTS

    pi = iota((FETCH, FETCH), 0)
    pb = pi // SLOTS
    perm = onehot(((pb % 8) * 8 + pb // 8) * SLOTS + pi % SLOTS == iota((FETCH, FETCH), 1))

    wait_all(copies)

    allreq = rq[...].reshape(NXC * NZ * 8, E)
    req_hi = (allreq // 64).astype(F32).astype(BF16)
    req_lo = (allreq % 64).astype(F32).astype(BF16)
    si = iota((FETCH, NXC * NZ * 8), 0)
    sb = si // SLOTS
    s_z = sb // NXC
    s_xc = sb % NXC
    s_row = (s_xc * NZ + s_z) * 8 + (si % SLOTS) // 2
    s_col = iota((FETCH, NXC * NZ * 8), 1)
    li = iota((FETCH, E), 0) % SLOTS
    lane_mask = iota((FETCH, E), 1) == (li % 2) * 64 + owner
    ones8 = jnp.ones((16, E), BF16)
    for t in range(STEPS):
        sel = onehot(s_row + 2 * t == s_col)
        hi = jnp.where(lane_mask, nn(sel, req_hi), 0.0)
        lo = jnp.where(lane_mask, nn(sel, req_lo), 0.0)
        col = jnp.sum(hi * 64.0 + lo, axis=1, keepdims=True)
        wcol[t] = jnp.broadcast_to(col, (FETCH, E)).astype(jnp.int32)
        row = nt(ones8, hi.astype(BF16)) * 64.0 + nt(ones8, lo.astype(BF16))
        wrow[t] = row[0:8].astype(jnp.int32)

    eye_e = onehot(iota((E, E), 0) == iota((E, E), 1))

    def step(t, carry):
        def gather(j, rows):
            at = al(j * CH, CH)
            want = wcol[t]
            lanes = iota((FETCH, E), 1) + j * CH
            r = jnp.concatenate([onehot(want == lanes), onehot(want == lanes + E)], axis=1)
            return rows + nn(r, table[pl.ds(at, CH), :].astype(BF16))

        s1[t] = lax.fori_loop(0, ROWS // CH, gather, jnp.zeros((FETCH, E), F32)).astype(BF16)

        def exchange(src, dst, n, me, peer, ssem, rsem):
            copies = []
            for k in range(1, n):
                p, d = peer(k)
                copies.append(remote(
                    src.at[t, pl.ds(al(p * SLAB, SLAB), SLAB)],
                    dst.at[t, pl.ds(al(me * SLAB, SLAB), SLAB)],
                    ssem.at[t, k], rsem.at[t, k], d,
                ))
            mine = pl.ds(al(me * SLAB, SLAB), SLAB)
            dst[t, mine] = src[t, mine]
            wait_all(copies)

        exchange(s1, r1, NZ, z, zpeer, f1s, f1r)
        s2[t] = nn(perm, r1[t]).astype(BF16)
        exchange(s2, r2, NXC, xc, xcpeer, f2s, f2r)
        fetched_t = nt(eye_e, r2[t]).astype(BF16)

        def pool(i, low):
            rows = mem[t, pl.ds(al(i * 8, 8), 8), :]
            pos = posq[...]
            cnt = []
            for b in range(2):
                n = jnp.where(pos == rows[4 * b:4 * b + 1, :], 1.0, 0.0)
                for m in range(1, BAGLEN):
                    n = n + jnp.where(pos == rows[4 * b + m:4 * b + m + 1, :], 1.0, 0.0)
                cnt.append(n.astype(BF16))
            both = jnp.concatenate(cnt, axis=1)
            counts[i] = both
            xx = nn(fetched_t, both).astype(BF16)
            xx = jnp.concatenate([xx[:, :TOK], xx[:, TOK:]], axis=0)
            at = al(i * CH, CH)
            x0s[t, pl.ds(at, CH), :] = xx
            return low + nn(down_t[:, pl.ds(at, CH)], xx)

        low = lax.fori_loop(0, NCH, pool, jnp.zeros((RANK, TOK), F32)).astype(BF16)
        lows[t] = low

        def forward(i, logit):
            at = al(i * CH, CH)
            gate = nn(up_t[pl.ds(at, CH), :], low) + bias_b[pl.ds(at, CH), :]
            gates[pl.ds(at, CH), :] = gate
            x0f = x0s[t, pl.ds(at, CH), :].astype(F32)
            x1 = (x0f * gate + x0f).astype(BF16)
            x1s[pl.ds(at, CH), :] = x1
            prod = x1.astype(F32) * out_b[pl.ds(at, CH), :]
            return logit + jnp.sum(prod.reshape(CH // 8, 8, TOK), axis=0)

        logit = lax.fori_loop(0, NCH, forward, jnp.zeros((8, TOK), F32))
        logit = jnp.sum(logit, axis=0, keepdims=True)
        dlogit = jax.nn.sigmoid(logit) - labels[pl.ds(t, 1), :].astype(F32)
        dhi = dlogit.astype(BF16).astype(F32)
        dmid = (dlogit - dhi).astype(BF16).astype(F32)
        dlo = dlogit - dhi - dmid
        sub = iota((16, TOK), 0)
        heads = jnp.where(sub == 0, dhi, jnp.where(sub == 1, dmid, jnp.where(sub == 2, dlo, 1.0)))
        heads = heads.astype(BF16)

        def backward(i, dlow):
            at = al(i * CH, CH)
            x0f = x0s[t, pl.ds(at, CH), :].astype(F32)
            dg = (dlogit * out_b[pl.ds(at, CH), :] * x0f).astype(BF16)
            dgs[t, pl.ds(at, CH), :] = dg
            bo3[0, i] = bo3[0, i] + nt(heads, dg)
            bo3[1, i] = bo3[1, i] + nt(heads, x1s[pl.ds(at, CH), :])
            return dlow + nn(up[:, pl.ds(at, CH)], dg)

        dlow = lax.fori_loop(0, NCH, backward, jnp.zeros((RANK, TOK), F32)).astype(BF16)
        dlows[t] = dlow

        def spread(i, gf):
            at = al(i * CH, CH)
            dx0 = dlogit * out_b[pl.ds(at, CH), :] * (gates[pl.ds(at, CH), :] + 1.0)
            dx0 = (dx0 + nn(down[pl.ds(at, CH), :], dlow)).astype(BF16)
            both = jnp.concatenate([dx0[:E], dx0[E:]], axis=1)
            return gf + nt(counts[i], both)

        g0[t] = lax.fori_loop(0, NCH, spread, jnp.zeros((FETCH, E), F32)).astype(BF16)
        exchange(g0, g1, NXC, xc, xcpeer, b1s, b1r)
        g2[t] = nn(perm, g1[t]).astype(BF16)
        exchange(g2, g3, NZ, z, zpeer, b2s, b2r)

        arrived = g3[t]

        def update(j, carry):
            at = al(j * CH, CH)
            want = wrow[t][0:1, :]
            rt = onehot(iota((CH, FETCH), 0) + j * CH == want)
            rg = nn(rt, arrived)
            acc = acc_b[pl.ds(at, CH), :] + jnp.mean(rg * rg, axis=1, keepdims=True)
            acc_b[pl.ds(at, CH), :] = acc
            table[pl.ds(at, CH), :] = table[pl.ds(at, CH), :] - learn_rate * rg * lax.rsqrt(acc)
            return carry

        lax.fori_loop(0, ROWS // CH, update, 0)
        return carry

    lax.fori_loop(0, STEPS, step, 0)

    def acc_rows(i, carry):
        at = al(i * E, E)
        accum_out[pl.ds(i, 1), :] = acc_b[pl.ds(at, E), :].T[0:1, :]
        return carry

    lax.fori_loop(0, ROWS // E, acc_rows, 0)

    bo[...] = jnp.zeros_like(bo)
    for i in range(NCH):
        b_row = bo3[0, i][3:4, :]
        o_rows = bo3[1, i]
        o_row = o_rows[0:1, :] + o_rows[1:2, :] + o_rows[2:3, :]
        for h in range(2):
            bo[0, 2 * i + h:2 * i + h + 1, :] = b_row[:, h * E:(h + 1) * E]
            bo[0, 32 + 2 * i + h:33 + 2 * i + h, :] = o_row[:, h * E:(h + 1) * E]
    bo_copy = remote(bo.at[0], boc, bcs, bcr, partner)

    dl_all = jnp.concatenate([dlows[t] for t in range(STEPS)], axis=1)
    lo_all = jnp.concatenate([lows[t] for t in range(STEPS)], axis=1)

    def dense(px, half):
        at = al(px * XROWS + half * HALF, 16)
        xx = jnp.concatenate([x0s[t, pl.ds(at, HALF), :] for t in range(STEPS)], axis=1)
        dd = jnp.concatenate([dgs[t, pl.ds(at, HALF), :] for t in range(STEPS)], axis=1)
        return nt(xx, dl_all), nt(dd, lo_all)

    core_copies = []
    for i in range(NX):
        px = (x + 1 + i) % NX
        gd, gu = dense(px, 1 - c)
        gs[i, :, 0:RANK] = gd.astype(BF16)
        gs[i, :, RANK:] = gu.astype(BF16)
        core_copies.append(remote(gs.at[i], rc.at[i], cs.at[i], cr.at[i], partner))

    x_copies, y_copies = [], []
    for i in range(NX):
        px = (x + 1 + i) % NX
        gd, gu = dense(px, c)
        core_copies[i].wait()
        ss[i, :, 0:RANK] = (gd + rc[i, :, 0:RANK].astype(F32)).astype(BF16)
        ss[i, :, RANK:] = (gu + rc[i, :, RANK:].astype(F32)).astype(BF16)
        if i < NX - 1:
            x_copies.append(remote(
                ss.at[i, pl.ds(0, PART)], rx1.at[i], xs.at[i], xr.at[i], xpeer(i + 1)[1]
            ))
        for k in range(1, NY):
            py, d = ypeer(k)
            y_copies.append(remote(
                ss.at[i, pl.ds(PART, PART), pl.ds(al(py * E, E), E)], ry1.at[k - 1, i],
                ys.at[i, k], yr.at[i, k], d,
            ))
    bo_copy.wait()
    bo[1] = bo[0] + boc[...]
    bx_copies = [remote(bo.at[1], box.at[k - 1], bxs.at[k], bxr.at[k], xpeer(k)[1]) for k in range(1, NX)]

    my_y = pl.ds(al(y * E, E), E)
    wait_all(x_copies)
    aa[...] = (
        ss[NX - 1, 0:PART, :].astype(F32) + rx1[0].astype(F32) + rx1[1].astype(F32) + rx1[2].astype(F32)
    ).astype(BF16)
    y2_copies = []
    for k in range(1, NY):
        py, d = ypeer(k)
        y2_copies.append(remote(
            aa.at[:, pl.ds(al(py * E, E), E)], ry2.at[k - 1], y2s.at[k], y2r.at[k], d
        ))
    wait_all(y_copies)
    for i in range(NX):
        bb[i] = (
            ss[i, PART:, my_y].astype(F32)
            + ry1[0, i].astype(F32) + ry1[1, i].astype(F32) + ry1[2, i].astype(F32)
        ).astype(BF16)
    x2_copies = []
    for k in range(1, NX):
        x2_copies.append(remote(bb.at[k - 1], rx2.at[k - 1], x2s.at[k], x2r.at[k], xpeer(k)[1]))
    wait_all(bx_copies)
    bo[2] = bo[1] + box[0] + box[1] + box[2]
    by_copies = [remote(bo.at[2], boy.at[k - 1], bys.at[k], byr.at[k], ypeer(k)[1]) for k in range(1, NY)]

    wait_all(y2_copies)
    ff[0:PART] = (
        aa[:, my_y].astype(F32) + ry2[0].astype(F32) + ry2[1].astype(F32) + ry2[2].astype(F32)
    )
    wait_all(x2_copies)
    ff[PART:] = (
        bb[NX - 1].astype(F32) + rx2[0].astype(F32) + rx2[1].astype(F32) + rx2[2].astype(F32)
    )

    def z_copy(k):
        zt = c * (NZ // NC) + k
        return pltpu.make_async_remote_copy(
            src_ref=ff.at[pl.ds(k * BLOCK, BLOCK)], dst_ref=rz.at[z],
            send_sem=zs.at[k], recv_sem=zr.at[z],
            device_id=dev(x, zt, c, y), device_id_type=pl.DeviceIdType.MESH,
        )

    for k in range(NZ // NC):
        zt = c * (NZ // NC) + k

        @pl.when(zt != z)
        def _():
            z_copy(k).start()

        @pl.when(zt == z)
        def _():
            rz[z] = ff[k * BLOCK:(k + 1) * BLOCK]

    wait_all(by_copies)
    bo[3] = bo[2] + boy[0] + boy[1] + boy[2]
    bz_copies = [remote(bo.at[3], boz.at[k - 1], bzs.at[k], bzr.at[k], zpeer(k)[1]) for k in range(1, NZ)]

    holder = z // (NZ // NC)

    @pl.when(holder == c)
    def _():
        for s in range(NZ):
            @pl.when(s != z)
            def _():
                pltpu.make_async_remote_copy(
                    src_ref=ff.at[pl.ds(0, BLOCK)], dst_ref=rz.at[s],
                    send_sem=zs.at[0], recv_sem=zr.at[s],
                    device_id=partner, device_id_type=pl.DeviceIdType.MESH,
                ).wait_recv()
        total = rz[0]
        for s in range(1, NZ):
            total = total + rz[s]
        tt[...] = total

    def window(pc, py):
        off = pc * (SHARE * NY) + py * SHARE
        first = jnp.minimum((off // 8) * 8, BLOCK - WIN)
        return al(first, 8), off - first

    def f_copy(k, h):
        py = (y + k) % NY
        pc = (c + h) % NC
        return pltpu.make_async_remote_copy(
            src_ref=tt.at[pl.ds(window(pc, py)[0], WIN)], dst_ref=fw.at[y],
            send_sem=fs.at[2 * k + h], recv_sem=fr.at[k],
            device_id=dev(x, z, pc, py), device_id_type=pl.DeviceIdType.MESH,
        )

    first, skip = window(c, y)

    @pl.when(holder == c)
    def _():
        for k in range(NY):
            for h in range(NC):
                if k or h:
                    f_copy(k, h).start()
        fw[y] = tt[pl.ds(first, WIN)]

    @pl.when(holder != c)
    def _():
        f_copy(0, 1).wait_recv()

    for k in range(1, NY):
        f_copy(k, 0).wait_recv()

    scale = 1.0 / (STEPS * TOK * NX * NY * NZ * NC)
    for py in range(NY):
        gdu_out[:, py * E:(py + 1) * E] = (
            pltpu.roll(fw[py], (WIN - skip) % WIN, 0)[0:16, :] * scale
        )

    wait_all(bz_copies)
    total = bo[3]
    for k in range(NZ - 1):
        total = total + boz[k]
    bo[4] = total * scale
    start = (owner * NY + y) * SHARE
    a = start // E
    rows = []
    for base in (0, 32):
        pair = jnp.concatenate([bo[4, pl.ds(base + a, 1), :], bo[4, pl.ds(base + a + 1, 1), :]], axis=1)
        pair = jnp.broadcast_to(pair, (8, 2 * E))
        rows.append(pltpu.roll(pair, (2 * E - start % E) % (2 * E), 1)[:, 0:E])
    bo_out[...] = jnp.where(iota((8, E), 0) == 0, rows[0], rows[1])

    for k in range(NZ // NC):
        @pl.when(c * (NZ // NC) + k != z)
        def _():
            z_copy(k).wait_send()

    @pl.when(holder == c)
    def _():
        for k in range(NY):
            for h in range(NC):
                if k or h:
                    f_copy(k, h).wait_send()


def local(table, accum, requests, members, labels, down_proj, up_proj, cross_bias, out_weight):
    reqs = jnp.transpose(requests[:, 0, 0], (0, 2, 1)).reshape(2 * STEPS, E)
    reqs = jnp.pad(reqs, ((0, 2), (0, 0)))
    mem = jnp.transpose(members, (0, 2, 3, 1)).reshape(STEPS, NB * BAGLEN, TOK)
    dma = pltpu.SemaphoreType.DMA
    vm = pltpu.VMEM
    scratch = [
        vm((NXC, NZ, 8, E), jnp.int32),
        vm((STEPS, FETCH, E), jnp.int32),
        vm((STEPS, 8, FETCH), jnp.int32),
    ]
    scratch += [vm((STEPS, FETCH, E), BF16)] * 8
    scratch += [
        vm((RANK, D_IN), BF16), vm((D_IN, RANK), BF16),
        vm((D_IN, TOK), F32), vm((D_IN, TOK), F32), vm((ROWS, E), F32), vm((FETCH, E), jnp.int32),
        vm((NCH, FETCH, 2 * TOK), BF16),
        vm((STEPS, D_IN, TOK), BF16), vm((STEPS, D_IN, TOK), BF16),
        vm((STEPS, RANK, TOK), BF16), vm((STEPS, RANK, TOK), BF16),
        vm((D_IN, TOK), F32), vm((D_IN, TOK), BF16), vm((2, NCH, 16, CH), F32),
        vm((NX, HALF, 2 * RANK), BF16), vm((NX, HALF, 2 * RANK), BF16), vm((NX, HALF, 2 * RANK), BF16),
        vm((NX - 1, PART, 2 * RANK), BF16), vm((NY - 1, NX, PART, E), BF16),
        vm((NX - 1, PART, E), BF16), vm((NY - 1, PART, E), BF16),
        vm((PART, 2 * RANK), BF16), vm((NX, PART, E), BF16), vm((HALF, E), F32),
        vm((NZ, BLOCK, E), F32), vm((BLOCK, E), F32), vm((NY, WIN, E), F32),
        vm((5, 64, E), F32), vm((64, E), F32), vm((NX - 1, 64, E), F32),
        vm((NY - 1, 64, E), F32), vm((NZ - 1, 64, E), F32),
    ]
    scratch += [dma((8,))] * 4
    scratch += [dma((STEPS, 8))] * 8
    scratch += [dma((NX,))] * 2
    scratch += [dma((NX,))] * 2
    scratch += [dma((NX, NY))] * 2
    scratch += [dma((NX,))] * 4
    scratch += [dma((NZ,))] * 2
    scratch += [dma((8,))] * 2
    scratch += [dma] * 2
    scratch += [dma((8,))] * 6
    spec = pl.BlockSpec(memory_space=pltpu.VMEM)
    table_new, accum_new, gdu, bo = pl.pallas_call(
        kernel,
        out_shape=(
            jax.ShapeDtypeStruct((ROWS, E), F32),
            jax.ShapeDtypeStruct((ROWS // E, E), F32),
            jax.ShapeDtypeStruct((16, 2 * RANK), F32),
            jax.ShapeDtypeStruct((8, E), F32),
        ),
        in_specs=[spec] * 9,
        out_specs=(spec,) * 4,
        scratch_shapes=scratch,
        compiler_params=pltpu.CompilerParams(
            collective_id=0, has_side_effects=True, vmem_limit_bytes=58 * 1024 * 1024
        ),
    )(
        table, accum.reshape(ROWS // E, E), reqs, mem, labels, down_proj, up_proj,
        cross_bias.reshape(NB, E), out_weight.astype(F32).reshape(NB, E),
    )
    return (
        table_new,
        accum_new.reshape(ROWS),
        gdu[:SHARE, :RANK],
        gdu[:SHARE, RANK:].T,
        bo[0, :SHARE],
        bo[1, :SHARE],
    )


def solution(mesh):
    both = ("owner", "group")
    in_specs = (
        P(both, None), P(both), P(None, "owner", "group", None, None),
        P(None, both, None, None), P(None, both), P(), P(), P(), P(),
    )
    out_specs = (P(both, None), P(both), P(both, None), P(None, both), P(both), P(both))
    return jax.shard_map(local, mesh=mesh, in_specs=in_specs, out_specs=out_specs, check_vma=False)
```

time: 1630 us -> 188 us (0.12)
  blocking collectives: 750 us -> 0 us
  starting transfers between devices: 630 us -> 0 us
  Pallas kernels: 0 us -> 177 us
  local copies, waits for them, and re-layouts: 90.6 us -> 6.85 us
  matrix products: 60.6 us -> 0 us
  waiting for transfers between devices: 48.4 us -> 0 us
  other arithmetic: 28.9 us -> 1.3 us
    unnamed x2 -> x0, blocking collectives: 750 us -> none
    unnamed x96 -> x0, starting transfers between devices: 569 us -> none
    pallas_call x0 -> x1, Pallas kernels: none -> 177 us  [local(): pl.pallas_call(kernel, out_shape=(jax.ShapeDtypeStruct((ROWS, E), F32), j...]
    all_to_all x9 -> x0, starting transfers between devices: 60.6 us -> none  [the longest x3 23.8 us: local(): lax.all_to_all(requests[step, 0, 0], 'owner', split_axis=0, concat_axis=0...]
    dot_general x27 -> x0, matrix products: 60.6 us -> none  [the longest x3 16.9 us: local(): pooled = jnp.dot(counts, fetched, preferred_element_type=jnp.float32)]
    unnamed x280 -> x4, local copies, waits for them, and re-layouts: 58.1 us -> 2.87 us
    all_to_all x9 -> x0, waiting for transfers between devices: 46.7 us -> none  [the longest x3 20.5 us: local(): lax.all_to_all(requests[step, 0, 0], 'owner', split_axis=0, concat_axis=0...]
  transfers between devices with their start and end apart: 105 -> 0, of which waited for: 9 -> 0; matrix products, arithmetic and copies ran while one was open for 6% -> 0% of each run, Pallas kernels for 0% -> 0%
where the time goes in v1:
time: 188 us; the launch traced here: 186 us
  Pallas kernels  177 us (94%)
  local copies, waits for them, and re-layouts  6.85 us (4%)
    pallas_call x1, Pallas kernels, local(): pl.pallas_call(kernel, out_shape=(jax.ShapeDtypeStruct((ROWS, E), F32), j...  177 us

profile of v1, /device:TPU:32, one launch (start us, length us, event | category | flops | bytes accessed | tf_op | source)
XLA Modules:
  0.0 185.9 jit_solution(4342997735175378313)
XLA Ops:
  0.6 1.3 bitcast_convert_fusion.outw
  1.9 0.8 reshape.33
  2.7 0.6 pad.4.reqs
  3.3 177.1 %shard_map.136 = (f32[2048,128]{1,0:T(8,128)}, f32[16,128]{1,0:T(8,128)}, f32[16,512]{1,0:T(8,128)}, f32[8,128]{1,0:T(8,128)}) custom-call(f32[2048,128]{1,0:T(8,128)} %table_in.1, f32[16,128]{1,0:T(8,128)} %bitcast.20, s32[8,128]{1,0:T(8,128)} %pad.4.reqs, s32[3,104,128]{2,1,0:T(8,128)} %bitcast.18, s32[3,128]{1,0:T(4,128)} %labels.1, ...), custom_call_target="tpu_custom_call" | custom-call | tf_op jit(solution)/shard_map/pallas_call | solution.py:529
  180.4 0.0 copy-start
  180.4 1.4 slice_bitcast_fusion
  181.8 1.3 slice_bitcast_fusion.1
  183.1 2.3 %copy.17 = f32[2048,128]{1,0:T(8,128)} copy(f32[2048,128]{1,0:T(8,128)} %get-tuple-element.24) | data formatting | bytes 2097152
  185.3 0.0 copy-done
  185.3 0.6 copy.18
Async XLA Ops:
  180.4 4.9 %copy-start = (f32[16,128]{1,0:T(8,128)S(1)}, f32[16,128]{1,0:T(8,128)}, u32[]{:S(2)}) copy-start(f32[16,128]{1,0:T(8,128)} %get-tuple-element.11) | copy-start | bytes 24580

commit v2 on v1

--- a/solution.py
+++ b/solution.py
@@ -8,7 +8,7 @@
 from jax.sharding import PartitionSpec as P
 
 NX, NY, NZ, NC = 4, 4, 8, 2
-NXC = NX * NC
+OWNERS = NX * NZ * NC
 NB = 26
 BAGLEN = 4
 STEPS = 3
@@ -18,10 +18,12 @@
 D_IN = NB * E
 ROWS = 2048
 SLOTS = 4
-FETCH = NZ * NXC * SLOTS
-SLAB = 32
+FETCH = OWNERS * SLOTS
 CH = 256
 NCH = D_IN // CH
+NROW = ROWS // CH
+UNROLL = 13
+UNROLL_ROWS = 4
 XROWS = D_IN // NX
 HALF = XROWS // NC
 PART = HALF // 2
@@ -69,71 +71,74 @@
 
 
 def kernel(
-    table_in, accum_in, reqs, mem, labels, down, up, bias, outw,
-    table, accum_out, gdu_out, bo_out,
-    rq, wcol, wrow, s1, r1, s2, r2, g0, g1, g2, g3,
+    table_in, accum_in, reqs, mem_in, labels, down_in, up_in, bias, outw,
+    table_hbm, accum_out, gdu_out, bo_out,
+    table, mem, down, up,
+    rqs, rqr, wcol, wrow, s1, r1, g1, g2, rr, rt,
     down_t, up_t, bias_b, out_b, acc_b, posq,
     counts, x0s, dgs, lows, dlows, gates, x1s, bo3,
     gs, rc, ss, rx1, ry1, rx2, ry2, aa, bb, ff, rz, tt, fw,
     bo, boc, box, boy, boz,
-    q1s, q1r, q2s, q2r, f1s, f1r, f2s, f2r, b1s, b1r, b2s, b2r,
+    lsem, qs, qr, s1s, s1r, g1s, g1r,
     cs, cr, xs, xr, ys, yr, x2s, x2r, y2s, y2r, zs, zr, fs, fr,
     bcs, bcr, bxs, bxr, bys, byr, bzs, bzr,
 ):
+    loads = [
+        pltpu.make_async_copy(src, dst, lsem.at[n])
+        for n, (src, dst) in enumerate(
+            ((down_in, down), (up_in, up), (mem_in, mem), (table_in, table))
+        )
+    ]
+    for load in loads:
+        load.start()
+
     owner = lax.axis_index("owner")
     y = lax.axis_index("group")
-    c = owner % NC
-    z = (owner // NC) % NZ
+    c = lax.rem(owner, NC)
+    z = lax.rem(owner // NC, NZ)
     x = owner // (NC * NZ)
-    xc = x * NC + c
+    at_x = [lax.rem(x + k, NX) for k in range(NX)]
+    at_z = [lax.rem(z + k, NZ) for k in range(NZ)]
+    at_y = [lax.rem(y + k, NY) for k in range(NY)]
+    at_c = [c, 1 - c]
 
     def dev(px, pz, pc, py):
         return ((px * NZ + pz) * NC + pc, py)
 
     def zpeer(k):
-        pz = (z + k) % NZ
-        return pz, dev(x, pz, c, y)
-
-    def xcpeer(k):
-        pxc = (xc + k) % NXC
-        return pxc, dev(pxc // NC, z, pxc % NC, y)
+        return at_z[k], dev(x, at_z[k], c, y)
 
     def xpeer(k):
-        px = (x + k) % NX
-        return px, dev(px, z, c, y)
+        return at_x[k], dev(at_x[k], z, c, y)
 
     def ypeer(k):
-        py = (y + k) % NY
-        return py, dev(x, z, c, py)
+        return at_y[k], dev(x, z, c, at_y[k])
 
     partner = dev(x, z, 1 - c, y)
+    far = [
+        (dx, dz, dc) for dx in range(NX) for dz in range(NZ) for dc in range(NC) if dx or dz or dc
+    ]
+    far.sort(key=lambda d: -(min(d[0], NX - d[0]) + min(d[1], NZ - d[1])))
+    users = [dev(at_x[dx], at_z[dz], at_c[dc], y) for dx, dz, dc in far]
 
     barrier = pltpu.get_barrier_semaphore()
-    greet = [zpeer(k)[1] for k in range(1, NZ)] + [xcpeer(k)[1] for k in range(1, NXC)]
-    greet += [ypeer(k)[1] for k in range(1, NY)]
-    greet += [dev(x, z, 1 - c, (y + k) % NY) for k in range(1, NY)]
+    greet = users + [dev(x, z, at_c[h], at_y[k]) for h in range(NC) for k in range(1, NY)]
     for peer in greet:
         pl.semaphore_signal(barrier, inc=1, device_id=peer, device_id_type=pl.DeviceIdType.MESH)
-    pl.semaphore_wait(barrier, len(greet))
-
-    rq[xc, z] = reqs[...]
-    copies = []
-    for k in range(1, NZ):
-        copies.append(remote(rq.at[xc, z], rq.at[xc, z], q1s.at[k], q1r.at[k], zpeer(k)[1]))
-
-    eye = onehot(iota((CH, CH), 0) == iota((CH, CH), 1))
-
-    def weights(i, carry):
-        at = al(i * CH, CH)
-        down_t[:, pl.ds(at, CH)] = nt(eye, down[pl.ds(at, CH), :]).astype(BF16)
-        up_t[pl.ds(at, CH), :] = nt(eye, up[:, pl.ds(at, CH)]).astype(BF16)
-        return carry
-
-    wait_all(copies)
-    copies = []
-    for k in range(1, NXC):
-        copies.append(remote(rq.at[xc], rq.at[xc], q2s.at[k], q2r.at[k], xcpeer(k)[1]))
-    lax.fori_loop(0, NCH, weights, 0)
+
+    def send_all(src, dst, ssem, rsem):
+        for peer in users:
+            remote(src.at[peer[0]], dst.at[owner], ssem, rsem, peer)
+
+    def sent_all(src, dst, ssem, rsem):
+        most = pl.ds(0, NX * NZ * NC - 1)
+        return pltpu.make_async_remote_copy(
+            src_ref=src.at[most], dst_ref=dst.at[most], send_sem=ssem, recv_sem=rsem,
+            device_id=partner, device_id_type=pl.DeviceIdType.MESH,
+        )
+
+    flat = jnp.concatenate([reqs[...].astype(F32), jnp.zeros((E - 16, E), F32)], axis=0).T
+    rqs[:, 0, :] = flat[0:OWNERS]
 
     def columns(i, carry):
         at = al(i * E, E)
@@ -141,81 +146,19 @@
         out_b[pl.ds(at, E), :] = jnp.broadcast_to(outw[pl.ds(i, 1), :], (E, E)).T
         return carry
 
-    lax.fori_loop(0, NB, columns, 0)
-
-    def acc_columns(i, carry):
-        at = al(i * E, E)
-        acc_b[pl.ds(at, E), :] = jnp.broadcast_to(accum_in[pl.ds(i, 1), :], (E, E)).T
-        return carry
-
-    lax.fori_loop(0, ROWS // E, acc_columns, 0)
-    table[...] = table_in[...]
-    bo3[...] = jnp.zeros_like(bo3)
+    lax.fori_loop(0, NB, columns, 0, unroll=2)
 
     qi = iota((FETCH, E), 0)
-    qb = qi // SLOTS
-    q_xc = qb // NZ
-    q_z = qb % NZ
-    posq[...] = (((q_xc // NC) * NZ + q_z) * NC + q_xc % NC) * SLOTS + qi % SLOTS
-
-    pi = iota((FETCH, FETCH), 0)
-    pb = pi // SLOTS
-    perm = onehot(((pb % 8) * 8 + pb // 8) * SLOTS + pi % SLOTS == iota((FETCH, FETCH), 1))
-
-    wait_all(copies)
-
-    allreq = rq[...].reshape(NXC * NZ * 8, E)
-    req_hi = (allreq // 64).astype(F32).astype(BF16)
-    req_lo = (allreq % 64).astype(F32).astype(BF16)
-    si = iota((FETCH, NXC * NZ * 8), 0)
-    sb = si // SLOTS
-    s_z = sb // NXC
-    s_xc = sb % NXC
-    s_row = (s_xc * NZ + s_z) * 8 + (si % SLOTS) // 2
-    s_col = iota((FETCH, NXC * NZ * 8), 1)
-    li = iota((FETCH, E), 0) % SLOTS
-    lane_mask = iota((FETCH, E), 1) == (li % 2) * 64 + owner
-    ones8 = jnp.ones((16, E), BF16)
-    for t in range(STEPS):
-        sel = onehot(s_row + 2 * t == s_col)
-        hi = jnp.where(lane_mask, nn(sel, req_hi), 0.0)
-        lo = jnp.where(lane_mask, nn(sel, req_lo), 0.0)
-        col = jnp.sum(hi * 64.0 + lo, axis=1, keepdims=True)
-        wcol[t] = jnp.broadcast_to(col, (FETCH, E)).astype(jnp.int32)
-        row = nt(ones8, hi.astype(BF16)) * 64.0 + nt(ones8, lo.astype(BF16))
-        wrow[t] = row[0:8].astype(jnp.int32)
-
+    posq[...] = lax.rem(qi, OWNERS) * SLOTS + qi // OWNERS
+    eye = onehot(iota((CH, CH), 0) == iota((CH, CH), 1))
     eye_e = onehot(iota((E, E), 0) == iota((E, E), 1))
 
-    def step(t, carry):
-        def gather(j, rows):
-            at = al(j * CH, CH)
-            want = wcol[t]
-            lanes = iota((FETCH, E), 1) + j * CH
-            r = jnp.concatenate([onehot(want == lanes), onehot(want == lanes + E)], axis=1)
-            return rows + nn(r, table[pl.ds(at, CH), :].astype(BF16))
-
-        s1[t] = lax.fori_loop(0, ROWS // CH, gather, jnp.zeros((FETCH, E), F32)).astype(BF16)
-
-        def exchange(src, dst, n, me, peer, ssem, rsem):
-            copies = []
-            for k in range(1, n):
-                p, d = peer(k)
-                copies.append(remote(
-                    src.at[t, pl.ds(al(p * SLAB, SLAB), SLAB)],
-                    dst.at[t, pl.ds(al(me * SLAB, SLAB), SLAB)],
-                    ssem.at[t, k], rsem.at[t, k], d,
-                ))
-            mine = pl.ds(al(me * SLAB, SLAB), SLAB)
-            dst[t, mine] = src[t, mine]
-            wait_all(copies)
-
-        exchange(s1, r1, NZ, z, zpeer, f1s, f1r)
-        s2[t] = nn(perm, r1[t]).astype(BF16)
-        exchange(s2, r2, NXC, xc, xcpeer, f2s, f2r)
-        fetched_t = nt(eye_e, r2[t]).astype(BF16)
-
-        def pool(i, low):
+    pl.semaphore_wait(barrier, len(greet))
+    send_all(rqs, rqr, qs.at[0], qr.at[0])
+    rqr[owner] = rqs[owner]
+
+    def count(t):
+        def bags(i, carry):
             rows = mem[t, pl.ds(al(i * 8, 8), 8), :]
             pos = posq[...]
             cnt = []
@@ -224,15 +167,90 @@
                 for m in range(1, BAGLEN):
                     n = n + jnp.where(pos == rows[4 * b + m:4 * b + m + 1, :], 1.0, 0.0)
                 cnt.append(n.astype(BF16))
-            both = jnp.concatenate(cnt, axis=1)
-            counts[i] = both
-            xx = nn(fetched_t, both).astype(BF16)
+            counts[lax.rem(t, 2), i] = jnp.concatenate(cnt, axis=1)
+            return carry
+
+        lax.fori_loop(0, NCH, bags, 0)
+
+    loads[0].wait()
+    loads[1].wait()
+
+    def weights(i, carry):
+        at = al(i * CH, CH)
+        down_t[:, pl.ds(at, CH)] = nt(eye, down[pl.ds(at, CH), :]).astype(BF16)
+        up_t[pl.ds(at, CH), :] = nt(eye, up[:, pl.ds(at, CH)]).astype(BF16)
+        return carry
+
+    lax.fori_loop(0, NCH, weights, 0)
+
+    def acc_columns(i, carry):
+        at = al(i * E, E)
+        acc_b[pl.ds(at, E), :] = jnp.broadcast_to(accum_in[pl.ds(i, 1), :], (E, E)).T
+        return carry
+
+    lax.fori_loop(0, ROWS // E, acc_columns, 0, unroll=2)
+    bo3[...] = jnp.zeros_like(bo3)
+    loads[2].wait()
+    count(0)
+
+    sent_all(rqs, rqr, qs.at[0], qr.at[0]).wait_recv()
+    arrived = rqr[:, 0, :]
+    for t in range(STEPS):
+        cols = [
+            jnp.broadcast_to(arrived[:, t * SLOTS + s:t * SLOTS + s + 1], (OWNERS, E))
+            for s in range(SLOTS)
+        ]
+        col = jnp.concatenate(cols, axis=0)
+        wcol[t] = col.astype(jnp.int32)
+        wrow[t] = col.T[0:8, :].astype(jnp.int32)
+
+    def pick(t):
+        def chunk(j, carry):
+            lanes = iota((FETCH, E), 1) + j * CH
+            want = wcol[t]
+            rr[j] = jnp.concatenate([onehot(want == lanes), onehot(want == lanes + E)], axis=1)
+            return carry
+
+        lax.fori_loop(0, NROW, chunk, 0)
+
+    def place(t):
+        def chunk(j, carry):
+            rt[j] = onehot(iota((CH, FETCH), 0) + j * CH == wrow[t][0:1, :])
+            return carry
+
+        lax.fori_loop(0, NROW, chunk, 0)
+
+    def put(dst, t, rows):
+        for s in range(SLOTS):
+            dst[t, :, s, :] = rows[s * OWNERS:(s + 1) * OWNERS]
+
+    def take(src, t):
+        return jnp.concatenate([src[t, :, s, :] for s in range(SLOTS)], axis=0)
+
+    pick(0)
+    loads[3].wait()
+    rows = jnp.zeros((FETCH, E), F32)
+    for j in range(NROW):
+        rows = rows + nn(rr[j], table[j * CH:(j + 1) * CH, :].astype(BF16))
+    put(s1, 0, rows)
+
+    def step(t, carry):
+        send_all(s1.at[t], r1.at[t], s1s.at[t], s1r.at[t])
+        r1[t, owner] = s1[t, owner]
+        place(t)
+        pick(jnp.minimum(t + 1, STEPS - 1))
+        cur = lax.rem(t, 2)
+        sent_all(s1.at[t], r1.at[t], s1s.at[t], s1r.at[t]).wait_recv()
+        fetched_t = nt(eye_e, take(r1, t).astype(BF16)).astype(BF16)
+
+        def pool(i, low):
+            xx = nn(fetched_t, counts[cur, i]).astype(BF16)
             xx = jnp.concatenate([xx[:, :TOK], xx[:, TOK:]], axis=0)
             at = al(i * CH, CH)
             x0s[t, pl.ds(at, CH), :] = xx
             return low + nn(down_t[:, pl.ds(at, CH)], xx)
 
-        low = lax.fori_loop(0, NCH, pool, jnp.zeros((RANK, TOK), F32)).astype(BF16)
+        low = lax.fori_loop(0, NCH, pool, jnp.zeros((RANK, TOK), F32), unroll=UNROLL).astype(BF16)
         lows[t] = low
 
         def forward(i, logit):
@@ -245,7 +263,7 @@
             prod = x1.astype(F32) * out_b[pl.ds(at, CH), :]
             return logit + jnp.sum(prod.reshape(CH // 8, 8, TOK), axis=0)
 
-        logit = lax.fori_loop(0, NCH, forward, jnp.zeros((8, TOK), F32))
+        logit = lax.fori_loop(0, NCH, forward, jnp.zeros((8, TOK), F32), unroll=UNROLL)
         logit = jnp.sum(logit, axis=0, keepdims=True)
         dlogit = jax.nn.sigmoid(logit) - labels[pl.ds(t, 1), :].astype(F32)
         dhi = dlogit.astype(BF16).astype(F32)
@@ -264,7 +282,7 @@
             bo3[1, i] = bo3[1, i] + nt(heads, x1s[pl.ds(at, CH), :])
             return dlow + nn(up[:, pl.ds(at, CH)], dg)
 
-        dlow = lax.fori_loop(0, NCH, backward, jnp.zeros((RANK, TOK), F32)).astype(BF16)
+        dlow = lax.fori_loop(0, NCH, backward, jnp.zeros((RANK, TOK), F32), unroll=UNROLL).astype(BF16)
         dlows[t] = dlow
 
         def spread(i, gf):
@@ -272,29 +290,39 @@
             dx0 = dlogit * out_b[pl.ds(at, CH), :] * (gates[pl.ds(at, CH), :] + 1.0)
             dx0 = (dx0 + nn(down[pl.ds(at, CH), :], dlow)).astype(BF16)
             both = jnp.concatenate([dx0[:E], dx0[E:]], axis=1)
-            return gf + nt(counts[i], both)
-
-        g0[t] = lax.fori_loop(0, NCH, spread, jnp.zeros((FETCH, E), F32)).astype(BF16)
-        exchange(g0, g1, NXC, xc, xcpeer, b1s, b1r)
-        g2[t] = nn(perm, g1[t]).astype(BF16)
-        exchange(g2, g3, NZ, z, zpeer, b2s, b2r)
-
-        arrived = g3[t]
-
-        def update(j, carry):
+            return gf + nt(counts[cur, i], both)
+
+        put(g1, t, lax.fori_loop(0, NCH, spread, jnp.zeros((FETCH, E), F32), unroll=UNROLL))
+        send_all(g1.at[t], g2.at[t], g1s.at[t], g1r.at[t])
+        g2[t, owner] = g1[t, owner]
+
+        @pl.when(t < STEPS - 1)
+        def _():
+            count(t + 1)
+
+        sent_all(g1.at[t], g2.at[t], g1s.at[t], g1r.at[t]).wait_recv()
+        back = take(g2, t)
+        hi = back.astype(BF16)
+        pair = jnp.concatenate([hi, (back - hi.astype(F32)).astype(BF16)], axis=1)
+
+        def update(j, rows):
             at = al(j * CH, CH)
-            want = wrow[t][0:1, :]
-            rt = onehot(iota((CH, FETCH), 0) + j * CH == want)
-            rg = nn(rt, arrived)
+            rg = nn(rt[j], pair)
+            rg = rg[:, :E] + rg[:, E:]
             acc = acc_b[pl.ds(at, CH), :] + jnp.mean(rg * rg, axis=1, keepdims=True)
             acc_b[pl.ds(at, CH), :] = acc
-            table[pl.ds(at, CH), :] = table[pl.ds(at, CH), :] - learn_rate * rg * lax.rsqrt(acc)
-            return carry
-
-        lax.fori_loop(0, ROWS // CH, update, 0)
+            new = table[pl.ds(at, CH), :] - learn_rate * rg * lax.rsqrt(acc)
+            table[pl.ds(at, CH), :] = new
+            return rows + nn(rr[j], new.astype(BF16))
+
+        rows = lax.fori_loop(0, NROW, update, jnp.zeros((FETCH, E), F32), unroll=UNROLL_ROWS)
+        put(s1, t + 1, rows)
         return carry
 
     lax.fori_loop(0, STEPS, step, 0)
+
+    store = pltpu.make_async_copy(table, table_hbm, lsem.at[0])
+    store.start()
 
     def acc_rows(i, carry):
         at = al(i * E, E)
@@ -487,23 +515,32 @@
                 if k or h:
                     f_copy(k, h).wait_send()
 
+    sent_all(rqs, rqr, qs.at[0], qr.at[0]).wait_send()
+    for t in range(STEPS):
+        sent_all(s1.at[t], r1.at[t], s1s.at[t], s1r.at[t]).wait_send()
+        sent_all(g1.at[t], g2.at[t], g1s.at[t], g1r.at[t]).wait_send()
+    store.wait()
+
 
 def local(table, accum, requests, members, labels, down_proj, up_proj, cross_bias, out_weight):
-    reqs = jnp.transpose(requests[:, 0, 0], (0, 2, 1)).reshape(2 * STEPS, E)
-    reqs = jnp.pad(reqs, ((0, 2), (0, 0)))
+    reqs = jnp.transpose(requests[:, 0, 0], (0, 2, 1)).reshape(STEPS * SLOTS, OWNERS)
+    reqs = jnp.pad(reqs, ((0, 4), (0, E - OWNERS)))
     mem = jnp.transpose(members, (0, 2, 3, 1)).reshape(STEPS, NB * BAGLEN, TOK)
     dma = pltpu.SemaphoreType.DMA
     vm = pltpu.VMEM
     scratch = [
-        vm((NXC, NZ, 8, E), jnp.int32),
-        vm((STEPS, FETCH, E), jnp.int32),
-        vm((STEPS, 8, FETCH), jnp.int32),
+        vm((ROWS, E), F32), vm((STEPS, NB * BAGLEN, TOK), jnp.int32),
+        vm((D_IN, RANK), BF16), vm((RANK, D_IN), BF16),
+        vm((OWNERS, 1, E), F32), vm((OWNERS, 1, E), F32),
+        vm((STEPS, FETCH, E), jnp.int32), vm((STEPS, 8, FETCH), jnp.int32),
+        vm((STEPS + 1, OWNERS, SLOTS, E), F32),
     ]
-    scratch += [vm((STEPS, FETCH, E), BF16)] * 8
+    scratch += [vm((STEPS, OWNERS, SLOTS, E), F32)] * 3
     scratch += [
+        vm((NROW, FETCH, CH), BF16), vm((NROW, CH, FETCH), BF16),
         vm((RANK, D_IN), BF16), vm((D_IN, RANK), BF16),
         vm((D_IN, TOK), F32), vm((D_IN, TOK), F32), vm((ROWS, E), F32), vm((FETCH, E), jnp.int32),
-        vm((NCH, FETCH, 2 * TOK), BF16),
+        vm((2, NCH, FETCH, 2 * TOK), BF16),
         vm((STEPS, D_IN, TOK), BF16), vm((STEPS, D_IN, TOK), BF16),
         vm((STEPS, RANK, TOK), BF16), vm((STEPS, RANK, TOK), BF16),
         vm((D_IN, TOK), F32), vm((D_IN, TOK), BF16), vm((2, NCH, 16, CH), F32),
@@ -515,8 +552,8 @@
         vm((5, 64, E), F32), vm((64, E), F32), vm((NX - 1, 64, E), F32),
         vm((NY - 1, 64, E), F32), vm((NZ - 1, 64, E), F32),
     ]
-    scratch += [dma((8,))] * 4
-    scratch += [dma((STEPS, 8))] * 8
+    scratch += [dma((4,)), dma((1,)), dma((1,))]
+    scratch += [dma((STEPS,))] * 4
     scratch += [dma((NX,))] * 2
     scratch += [dma((NX,))] * 2
     scratch += [dma((NX, NY))] * 2
@@ -525,6 +562,7 @@
     scratch += [dma((8,))] * 2
     scratch += [dma] * 2
     scratch += [dma((8,))] * 6
+    hbm = pl.BlockSpec(memory_space=pl.ANY)
     spec = pl.BlockSpec(memory_space=pltpu.VMEM)
     table_new, accum_new, gdu, bo = pl.pallas_call(
         kernel,
@@ -534,8 +572,8 @@
             jax.ShapeDtypeStruct((16, 2 * RANK), F32),
             jax.ShapeDtypeStruct((8, E), F32),
         ),
-        in_specs=[spec] * 9,
-        out_specs=(spec,) * 4,
+        in_specs=[hbm, spec, spec, hbm, spec, hbm, hbm, spec, spec],
+        out_specs=(hbm, spec, spec, spec),
         scratch_shapes=scratch,
         compiler_params=pltpu.CompilerParams(
             collective_id=0, has_side_effects=True, vmem_limit_bytes=58 * 1024 * 1024

time: 188 us -> 126 us (0.67)
  Pallas kernels: 177 us -> 117 us
    pallas_call x1, Pallas kernels: 177 us -> 117 us  [local(): pl.pallas_call(kernel, out_shape=(jax.ShapeDtypeStruct((ROWS, E), F32), j...]
where the time goes in v2:
time: 126 us; the launch traced here: 125 us
  Pallas kernels  117 us (93%)
  local copies, waits for them, and re-layouts  6.79 us (5%)
  other arithmetic  1.3 us (1%)
    pallas_call x1, Pallas kernels, local(): pl.pallas_call(kernel, out_shape=(jax.ShapeDtypeStruct((ROWS, E), F32), j...  117 us
    unnamed x4, local copies, waits for them, and re-layouts  2.87 us

profile of v2, /device:TPU:32, one launch (start us, length us, event | category | flops | bytes accessed | tf_op | source)
XLA Modules:
  0.0 125.3 jit_solution(1320781380480462062)
XLA Ops:
  0.6 1.3 %bitcast_convert_fusion.outw = f32[26,128]{1,0:T(8,128)} fusion(bf16[3328]{0:T(1024)(128)(2,1)} %param.17), kind=kLoop, calls=%fused_computation.1 | loop fusion | flops 3328 | bytes 19968 | tf_op jit(solution)/shard_map/reshape | solution.py:583
  1.9 0.7 reshape.33
  2.6 0.6 pad.4.reqs
  3.2 116.5 %shard_map.136 = (f32[2048,128]{1,0:T(8,128)}, f32[16,128]{1,0:T(8,128)}, f32[16,512]{1,0:T(8,128)}, f32[8,128]{1,0:T(8,128)}) custom-call(f32[2048,128]{1,0:T(8,128)} %table_in.1, f32[16,128]{1,0:T(8,128)} %bitcast.20, s32[16,128]{1,0:T(8,128)} %pad.4.reqs, s32[3,104,128]{2,1,0:T(8,128)} %bitcast.18, s32[3,128]{1,0:T(4,128)} %labels.1, ...), custom_call_target="tpu_custom_call" | custom-call | tf_op jit(solution)/shard_map/pallas_call | solution.py:567
  119.8 0.0 copy-start
  119.8 1.4 %slice_bitcast_fusion = (f32[256,13]{0,1:T(8,128)}, f32[13,256]{1,0:T(8,128)}) fusion(f32[16,512]{1,0:T(8,128)} %get-tuple-element.12), kind=kLoop, calls=%fused_computation | loop fusion | bytes 53248 | tf_op jit(solution)/shard_map/transpose | solution.py:589
  121.1 1.3 %slice_bitcast_fusion.1 = (f32[13]{0:T(128)}, f32[13]{0:T(128)}) fusion(f32[8,128]{1,0:T(8,128)} %get-tuple-element.13), kind=kLoop, calls=%fused_computation.2 | loop fusion | bytes 208 | tf_op jit(solution)/shard_map/squeeze | solution.py:591
  122.4 2.3 %copy.17 = f32[2048,128]{1,0:T(8,128)} copy(f32[2048,128]{1,0:T(8,128)} %get-tuple-element.24) | data formatting | bytes 2097152
  124.7 0.0 copy-done
  124.7 0.6 copy.18
Async XLA Ops:
  119.8 4.9 %copy-start = (f32[16,128]{1,0:T(8,128)S(1)}, f32[16,128]{1,0:T(8,128)}, u32[]{:S(2)}) copy-start(f32[16,128]{1,0:T(8,128)} %get-tuple-element.11) | copy-start | bytes 24580

commit v3 on v2

--- a/solution.py
+++ b/solution.py
@@ -25,11 +25,11 @@
 UNROLL = 13
 UNROLL_ROWS = 4
 XROWS = D_IN // NX
-HALF = XROWS // NC
-PART = HALF // 2
 BLOCK = XROWS // NZ
+HALF = BLOCK // NC
+GROUP = 64
+CORE_ROWS = NX * NZ * GROUP
 SHARE = 13
-WIN = 24
 
 learn_rate = 0.05
 F32 = jnp.float32
@@ -77,10 +77,10 @@
     rqs, rqr, wcol, wrow, s1, r1, g1, g2, rr, rt,
     down_t, up_t, bias_b, out_b, acc_b, posq,
     counts, x0s, dgs, lows, dlows, gates, x1s, bo3,
-    gs, rc, ss, rx1, ry1, rx2, ry2, aa, bb, ff, rz, tt, fw,
-    bo, boc, box, boy, boz,
+    xw, xo, dw, do, lowp, dlowp, sa, ra, sb, rb, a2, ra2, b2, rb2, z3, rz,
+    bo, boc, bw, bwx, bv, bvy, bvz,
     lsem, qs, qr, s1s, s1r, g1s, g1r,
-    cs, cr, xs, xr, ys, yr, x2s, x2r, y2s, y2r, zs, zr, fs, fr,
+    fs, fr, xs, xr, ys, yr, x2s, x2r, y2s, y2r, zs, zr,
     bcs, bcr, bxs, bxr, bys, byr, bzs, bzr,
 ):
     loads = [
@@ -234,6 +234,138 @@
         rows = rows + nn(rr[j], table[j * CH:(j + 1) * CH, :].astype(BF16))
     put(s1, 0, rows)
 
+    def copy_to(src, dst, send, recv, peer):
+        return pltpu.make_async_remote_copy(
+            src_ref=src, dst_ref=dst, send_sem=send, recv_sem=recv,
+            device_id=peer, device_id_type=pl.DeviceIdType.MESH,
+        )
+
+    def factors(t):
+        pairs = ((xo.at[t], xw.at[t, 1]), (do.at[t], dw.at[t, 1]),
+                 (lows.at[t], lowp.at[t]), (dlows.at[t], dlowp.at[t]))
+        return [copy_to(a, b, fs.at[t, n], fr.at[t, n], partner) for n, (a, b) in enumerate(pairs)]
+
+    def windows(t):
+        def one(i, carry):
+            to = pl.ds(al(i * GROUP, GROUP), GROUP)
+            mine = pl.ds(al((i * BLOCK + HALF * c) // 16 * 16, 16), GROUP)
+            other = pl.ds(al((i * BLOCK + HALF * (1 - c)) // 16 * 16, 16), GROUP)
+            xw[t, 0, to, :] = x0s[t, mine, :]
+            xo[t, to, :] = x0s[t, other, :]
+            dw[t, 0, to, :] = dgs[t, mine, :]
+            do[t, to, :] = dgs[t, other, :]
+            return carry
+
+        lax.fori_loop(0, NX * NZ, one, 0, unroll=4)
+        for copy in factors(t):
+            copy.start()
+
+    mi = iota((CH, CH), 0)
+    m_in = lax.rem(mi, 16)
+    m_off = lax.rem(mi // GROUP, 2) * 8 + 4 * c
+    m_col = mi // GROUP * GROUP + m_off + lax.rem(mi // 16, NY) * SHARE + m_in
+    spots = onehot((m_col == iota((CH, CH), 1)) & (m_in < SHARE))
+
+    def stage_x(k):
+        return copy_to(sa.at[k - 1], ra.at[k - 1], xs.at[k], xr.at[k], xpeer(k)[1])
+
+    def stage_y(i, k):
+        py, d = ypeer(k)
+        return copy_to(sb.at[py, i], rb.at[k - 1, i], ys.at[i, k], yr.at[i, k], d)
+
+    def stage_y2(k):
+        py, d = ypeer(k)
+        return copy_to(a2.at[py], ra2.at[k - 1], y2s.at[k], y2r.at[k], d)
+
+    def stage_x2(k):
+        return copy_to(b2.at[k - 1], rb2.at[k - 1], x2s.at[k], x2r.at[k], xpeer(k)[1])
+
+    def stage_z(k):
+        pz, d = zpeer(k)
+        return copy_to(z3.at[pl.ds(al(pz * 16, 16), 16)], rz.at[k - 1], zs.at[k], zr.at[k], d)
+
+    def bo_core():
+        return copy_to(bo.at[0], boc, bcs, bcr, partner)
+
+    def bo_x(k):
+        px, d = xpeer(k)
+        return copy_to(bw.at[px], bwx.at[k - 1], bxs.at[k], bxr.at[k], d)
+
+    def bo_y(k):
+        return copy_to(bv.at[0], bvy.at[k - 1], bys.at[k], byr.at[k], ypeer(k)[1])
+
+    def bo_z(k):
+        return copy_to(bv.at[1], bvz.at[k - 1], bzs.at[k], bzr.at[k], zpeer(k)[1])
+
+    def dense():
+        windows(STEPS - 1)
+        bo[...] = jnp.zeros_like(bo)
+        for i in range(NCH):
+            b_row = bo3[0, i][3:4, :]
+            o_rows = bo3[1, i]
+            o_row = o_rows[0:1, :] + o_rows[1:2, :] + o_rows[2:3, :]
+            for h in range(2):
+                bo[0, 2 * i + h:2 * i + h + 1, :] = b_row[:, h * E:(h + 1) * E]
+                bo[0, 32 + 2 * i + h:33 + 2 * i + h, :] = o_row[:, h * E:(h + 1) * E]
+        bo_core().start()
+        for t in range(STEPS):
+            for copy in factors(t):
+                copy.wait_recv()
+        dl = jnp.concatenate([r[t] for t in range(STEPS) for r in (dlows, dlowp)], axis=1)
+        lo = jnp.concatenate([r[t] for t in range(STEPS) for r in (lows, lowp)], axis=1)
+        for i in range(NX):
+            px = at_x[(i + 1) % NX]
+            for h in range(2):
+                rows = pl.ds(al((px * 2 + h) * CH, CH), CH)
+                xx = jnp.concatenate([xw[t, p, rows, :] for t in range(STEPS) for p in range(2)], axis=1)
+                dd = jnp.concatenate([dw[t, p, rows, :] for t in range(STEPS) for p in range(2)], axis=1)
+                g = jnp.concatenate([nt(xx, dl).astype(BF16), nt(dd, lo).astype(BF16)], axis=1)
+                g = nn(spots, g).astype(BF16)
+                for zl in range(NZ // 2):
+                    to = (h * (NZ // 2) + zl) * 16
+                    for py in range(NY):
+                        at = (zl * NY + py) * 16
+                        sa[i, py, to:to + 16, :] = g[at:at + 16, :RANK]
+                        sb[py, i, to:to + 16, :] = g[at:at + 16, RANK:]
+            if i < NX - 1:
+                stage_x(i + 1).start()
+            for k in range(1, NY):
+                stage_y(i, k).start()
+        bo_core().wait()
+        both = bo[0] + boc[...]
+        bo[1] = both
+        for px in range(NX):
+            first = px * XROWS // E
+            bw[px, 0:8, :] = bo[1, first:first + 8, :]
+            bw[px, 8:16, :] = bo[1, 32 + first:40 + first, :]
+        for k in range(1, NX):
+            bo_x(k).start()
+
+    def second():
+        for k in range(1, NX):
+            bo_x(k).wait()
+        bv[0] = bw[x] + bwx[0] + bwx[1] + bwx[2]
+        for k in range(1, NY):
+            bo_y(k).start()
+        for k in range(1, NX):
+            stage_x(k).wait()
+        for py in range(NY):
+            a2[py] = (
+                sa[NX - 1, py].astype(F32)
+                + ra[0, py].astype(F32) + ra[1, py].astype(F32) + ra[2, py].astype(F32)
+            ).astype(BF16)
+        for k in range(1, NY):
+            stage_y2(k).start()
+        for i in range(NX):
+            for k in range(1, NY):
+                stage_y(i, k).wait()
+            b2[i] = (
+                sb[y, i].astype(F32)
+                + rb[0, i].astype(F32) + rb[1, i].astype(F32) + rb[2, i].astype(F32)
+            ).astype(BF16)
+            if i < NX - 1:
+                stage_x2(i + 1).start()
+
     def step(t, carry):
         send_all(s1.at[t], r1.at[t], s1s.at[t], s1r.at[t])
         r1[t, owner] = s1[t, owner]
@@ -285,6 +417,10 @@
         dlow = lax.fori_loop(0, NCH, backward, jnp.zeros((RANK, TOK), F32), unroll=UNROLL).astype(BF16)
         dlows[t] = dlow
 
+        @pl.when(t == STEPS - 1)
+        def _():
+            dense()
+
         def spread(i, gf):
             at = al(i * CH, CH)
             dx0 = dlogit * out_b[pl.ds(at, CH), :] * (gates[pl.ds(at, CH), :] + 1.0)
@@ -299,6 +435,11 @@
         @pl.when(t < STEPS - 1)
         def _():
             count(t + 1)
+            windows(t)
+
+        @pl.when(t == STEPS - 1)
+        def _():
+            second()
 
         sent_all(g1.at[t], g2.at[t], g1s.at[t], g1r.at[t]).wait_recv()
         back = take(g2, t)
@@ -331,190 +472,50 @@
 
     lax.fori_loop(0, ROWS // E, acc_rows, 0)
 
-    bo[...] = jnp.zeros_like(bo)
-    for i in range(NCH):
-        b_row = bo3[0, i][3:4, :]
-        o_rows = bo3[1, i]
-        o_row = o_rows[0:1, :] + o_rows[1:2, :] + o_rows[2:3, :]
-        for h in range(2):
-            bo[0, 2 * i + h:2 * i + h + 1, :] = b_row[:, h * E:(h + 1) * E]
-            bo[0, 32 + 2 * i + h:33 + 2 * i + h, :] = o_row[:, h * E:(h + 1) * E]
-    bo_copy = remote(bo.at[0], boc, bcs, bcr, partner)
-
-    dl_all = jnp.concatenate([dlows[t] for t in range(STEPS)], axis=1)
-    lo_all = jnp.concatenate([lows[t] for t in range(STEPS)], axis=1)
-
-    def dense(px, half):
-        at = al(px * XROWS + half * HALF, 16)
-        xx = jnp.concatenate([x0s[t, pl.ds(at, HALF), :] for t in range(STEPS)], axis=1)
-        dd = jnp.concatenate([dgs[t, pl.ds(at, HALF), :] for t in range(STEPS)], axis=1)
-        return nt(xx, dl_all), nt(dd, lo_all)
-
-    core_copies = []
-    for i in range(NX):
-        px = (x + 1 + i) % NX
-        gd, gu = dense(px, 1 - c)
-        gs[i, :, 0:RANK] = gd.astype(BF16)
-        gs[i, :, RANK:] = gu.astype(BF16)
-        core_copies.append(remote(gs.at[i], rc.at[i], cs.at[i], cr.at[i], partner))
-
-    x_copies, y_copies = [], []
-    for i in range(NX):
-        px = (x + 1 + i) % NX
-        gd, gu = dense(px, c)
-        core_copies[i].wait()
-        ss[i, :, 0:RANK] = (gd + rc[i, :, 0:RANK].astype(F32)).astype(BF16)
-        ss[i, :, RANK:] = (gu + rc[i, :, RANK:].astype(F32)).astype(BF16)
-        if i < NX - 1:
-            x_copies.append(remote(
-                ss.at[i, pl.ds(0, PART)], rx1.at[i], xs.at[i], xr.at[i], xpeer(i + 1)[1]
-            ))
-        for k in range(1, NY):
-            py, d = ypeer(k)
-            y_copies.append(remote(
-                ss.at[i, pl.ds(PART, PART), pl.ds(al(py * E, E), E)], ry1.at[k - 1, i],
-                ys.at[i, k], yr.at[i, k], d,
-            ))
-    bo_copy.wait()
-    bo[1] = bo[0] + boc[...]
-    bx_copies = [remote(bo.at[1], box.at[k - 1], bxs.at[k], bxr.at[k], xpeer(k)[1]) for k in range(1, NX)]
-
-    my_y = pl.ds(al(y * E, E), E)
-    wait_all(x_copies)
-    aa[...] = (
-        ss[NX - 1, 0:PART, :].astype(F32) + rx1[0].astype(F32) + rx1[1].astype(F32) + rx1[2].astype(F32)
+    for k in range(1, NY):
+        bo_y(k).wait()
+    bv[1] = bv[0] + bvy[0] + bvy[1] + bvy[2]
+    for k in range(1, NZ):
+        bo_z(k).start()
+    for k in range(1, NY):
+        stage_y2(k).wait()
+    for k in range(1, NX):
+        stage_x2(k).wait()
+    z3[:, :RANK] = (
+        a2[y].astype(F32) + ra2[0].astype(F32) + ra2[1].astype(F32) + ra2[2].astype(F32)
     ).astype(BF16)
-    y2_copies = []
-    for k in range(1, NY):
-        py, d = ypeer(k)
-        y2_copies.append(remote(
-            aa.at[:, pl.ds(al(py * E, E), E)], ry2.at[k - 1], y2s.at[k], y2r.at[k], d
-        ))
-    wait_all(y_copies)
-    for i in range(NX):
-        bb[i] = (
-            ss[i, PART:, my_y].astype(F32)
-            + ry1[0, i].astype(F32) + ry1[1, i].astype(F32) + ry1[2, i].astype(F32)
-        ).astype(BF16)
-    x2_copies = []
-    for k in range(1, NX):
-        x2_copies.append(remote(bb.at[k - 1], rx2.at[k - 1], x2s.at[k], x2r.at[k], xpeer(k)[1]))
-    wait_all(bx_copies)
-    bo[2] = bo[1] + box[0] + box[1] + box[2]
-    by_copies = [remote(bo.at[2], boy.at[k - 1], bys.at[k], byr.at[k], ypeer(k)[1]) for k in range(1, NY)]
-
-    wait_all(y2_copies)
-    ff[0:PART] = (
-        aa[:, my_y].astype(F32) + ry2[0].astype(F32) + ry2[1].astype(F32) + ry2[2].astype(F32)
-    )
-    wait_all(x2_copies)
-    ff[PART:] = (
-        bb[NX - 1].astype(F32) + rx2[0].astype(F32) + rx2[1].astype(F32) + rx2[2].astype(F32)
-    )
-
-    def z_copy(k):
-        zt = c * (NZ // NC) + k
-        return pltpu.make_async_remote_copy(
-            src_ref=ff.at[pl.ds(k * BLOCK, BLOCK)], dst_ref=rz.at[z],
-            send_sem=zs.at[k], recv_sem=zr.at[z],
-            device_id=dev(x, zt, c, y), device_id_type=pl.DeviceIdType.MESH,
-        )
-
-    for k in range(NZ // NC):
-        zt = c * (NZ // NC) + k
-
-        @pl.when(zt != z)
-        def _():
-            z_copy(k).start()
-
-        @pl.when(zt == z)
-        def _():
-            rz[z] = ff[k * BLOCK:(k + 1) * BLOCK]
-
-    wait_all(by_copies)
-    bo[3] = bo[2] + boy[0] + boy[1] + boy[2]
-    bz_copies = [remote(bo.at[3], boz.at[k - 1], bzs.at[k], bzr.at[k], zpeer(k)[1]) for k in range(1, NZ)]
-
-    holder = z // (NZ // NC)
-
-    @pl.when(holder == c)
-    def _():
-        for s in range(NZ):
-            @pl.when(s != z)
-            def _():
-                pltpu.make_async_remote_copy(
-                    src_ref=ff.at[pl.ds(0, BLOCK)], dst_ref=rz.at[s],
-                    send_sem=zs.at[0], recv_sem=zr.at[s],
-                    device_id=partner, device_id_type=pl.DeviceIdType.MESH,
-                ).wait_recv()
-        total = rz[0]
-        for s in range(1, NZ):
-            total = total + rz[s]
-        tt[...] = total
-
-    def window(pc, py):
-        off = pc * (SHARE * NY) + py * SHARE
-        first = jnp.minimum((off // 8) * 8, BLOCK - WIN)
-        return al(first, 8), off - first
-
-    def f_copy(k, h):
-        py = (y + k) % NY
-        pc = (c + h) % NC
-        return pltpu.make_async_remote_copy(
-            src_ref=tt.at[pl.ds(window(pc, py)[0], WIN)], dst_ref=fw.at[y],
-            send_sem=fs.at[2 * k + h], recv_sem=fr.at[k],
-            device_id=dev(x, z, pc, py), device_id_type=pl.DeviceIdType.MESH,
-        )
-
-    first, skip = window(c, y)
-
-    @pl.when(holder == c)
-    def _():
-        for k in range(NY):
-            for h in range(NC):
-                if k or h:
-                    f_copy(k, h).start()
-        fw[y] = tt[pl.ds(first, WIN)]
-
-    @pl.when(holder != c)
-    def _():
-        f_copy(0, 1).wait_recv()
-
-    for k in range(1, NY):
-        f_copy(k, 0).wait_recv()
+    z3[:, RANK:] = (
+        b2[NX - 1].astype(F32) + rb2[0].astype(F32) + rb2[1].astype(F32) + rb2[2].astype(F32)
+    ).astype(BF16)
+    for k in range(1, NZ):
+        stage_z(k).start()
 
     scale = 1.0 / (STEPS * TOK * NX * NY * NZ * NC)
-    for py in range(NY):
-        gdu_out[:, py * E:(py + 1) * E] = (
-            pltpu.roll(fw[py], (WIN - skip) % WIN, 0)[0:16, :] * scale
-        )
-
-    wait_all(bz_copies)
-    total = bo[3]
+    for k in range(1, NZ):
+        bo_z(k).wait()
+    total = bv[1]
     for k in range(NZ - 1):
-        total = total + boz[k]
-    bo[4] = total * scale
-    start = (owner * NY + y) * SHARE
+        total = total + bvz[k]
+    bv[2] = total * scale
+    start = (owner * NY + y) * SHARE - (x * XROWS // E) * E
     a = start // E
     rows = []
-    for base in (0, 32):
-        pair = jnp.concatenate([bo[4, pl.ds(base + a, 1), :], bo[4, pl.ds(base + a + 1, 1), :]], axis=1)
+    for base in (0, 8):
+        pair = jnp.concatenate([bv[2, pl.ds(base + a, 1), :], bv[2, pl.ds(lax.rem(base + a + 1, 16), 1), :]], axis=1)
         pair = jnp.broadcast_to(pair, (8, 2 * E))
-        rows.append(pltpu.roll(pair, (2 * E - start % E) % (2 * E), 1)[:, 0:E])
+        rows.append(pltpu.roll(pair, lax.rem(2 * E - lax.rem(start, E), 2 * E), 1)[:, 0:E])
     bo_out[...] = jnp.where(iota((8, E), 0) == 0, rows[0], rows[1])
 
-    for k in range(NZ // NC):
-        @pl.when(c * (NZ // NC) + k != z)
-        def _():
-            z_copy(k).wait_send()
-
-    @pl.when(holder == c)
-    def _():
-        for k in range(NY):
-            for h in range(NC):
-                if k or h:
-                    f_copy(k, h).wait_send()
-
+    for k in range(1, NZ):
+        stage_z(k).wait()
+    total = z3[pl.ds(al(z * 16, 16), 16), :].astype(F32)
+    for k in range(NZ - 1):
+        total = total + rz[k].astype(F32)
+    gdu_out[...] = total * scale
+
+    for t in range(STEPS):
+        for copy in factors(t):
+            copy.wait_send()
     sent_all(rqs, rqr, qs.at[0], qr.at[0]).wait_send()
     for t in range(STEPS):
         sent_all(s1.at[t], r1.at[t], s1s.at[t], s1r.at[t]).wait_send()
@@ -544,22 +545,25 @@
         vm((STEPS, D_IN, TOK), BF16), vm((STEPS, D_IN, TOK), BF16),
         vm((STEPS, RANK, TOK), BF16), vm((STEPS, RANK, TOK), BF16),
         vm((D_IN, TOK), F32), vm((D_IN, TOK), BF16), vm((2, NCH, 16, CH), F32),
-        vm((NX, HALF, 2 * RANK), BF16), vm((NX, HALF, 2 * RANK), BF16), vm((NX, HALF, 2 * RANK), BF16),
-        vm((NX - 1, PART, 2 * RANK), BF16), vm((NY - 1, NX, PART, E), BF16),
-        vm((NX - 1, PART, E), BF16), vm((NY - 1, PART, E), BF16),
-        vm((PART, 2 * RANK), BF16), vm((NX, PART, E), BF16), vm((HALF, E), F32),
-        vm((NZ, BLOCK, E), F32), vm((BLOCK, E), F32), vm((NY, WIN, E), F32),
-        vm((5, 64, E), F32), vm((64, E), F32), vm((NX - 1, 64, E), F32),
-        vm((NY - 1, 64, E), F32), vm((NZ - 1, 64, E), F32),
+        vm((STEPS, 2, CORE_ROWS, TOK), BF16), vm((STEPS, CORE_ROWS, TOK), BF16),
+        vm((STEPS, 2, CORE_ROWS, TOK), BF16), vm((STEPS, CORE_ROWS, TOK), BF16),
+        vm((STEPS, RANK, TOK), BF16), vm((STEPS, RANK, TOK), BF16),
+        vm((NX, NY, NZ * 16, RANK), BF16), vm((NX - 1, NY, NZ * 16, RANK), BF16),
+        vm((NY, NX, NZ * 16, RANK), BF16), vm((NY - 1, NX, NZ * 16, RANK), BF16),
+        vm((NY, NZ * 16, RANK), BF16), vm((NY - 1, NZ * 16, RANK), BF16),
+        vm((NX, NZ * 16, RANK), BF16), vm((NX - 1, NZ * 16, RANK), BF16),
+        vm((NZ * 16, 2 * RANK), BF16), vm((NZ - 1, 16, 2 * RANK), BF16),
+        vm((2, 64, E), F32), vm((64, E), F32),
+        vm((NX, 16, E), F32), vm((NX - 1, 16, E), F32), vm((3, 16, E), F32),
+        vm((NY - 1, 16, E), F32), vm((NZ - 1, 16, E), F32),
     ]
     scratch += [dma((4,)), dma((1,)), dma((1,))]
     scratch += [dma((STEPS,))] * 4
-    scratch += [dma((NX,))] * 2
+    scratch += [dma((STEPS, 4))] * 2
     scratch += [dma((NX,))] * 2
     scratch += [dma((NX, NY))] * 2
     scratch += [dma((NX,))] * 4
     scratch += [dma((NZ,))] * 2
-    scratch += [dma((8,))] * 2
     scratch += [dma] * 2
     scratch += [dma((8,))] * 6
     hbm = pl.BlockSpec(memory_space=pl.ANY)

time: 126 us -> 113 us (0.90)
  Pallas kernels: 117 us -> 102 us
    pallas_call x1, Pallas kernels: 117 us -> 102 us  [local(): pl.pallas_call(kernel, out_shape=(jax.ShapeDtypeStruct((ROWS, E), F32), j...]
where the time goes in v3:
time: 113 us; the launch traced here: 111 us
  Pallas kernels  102 us (90%)
  local copies, waits for them, and re-layouts  6.79 us (6%)
  other arithmetic  1.3 us (1%)
    pallas_call x1, Pallas kernels, local(): pl.pallas_call(kernel, out_shape=(jax.ShapeDtypeStruct((ROWS, E), F32), j...  102 us
    unnamed x4, local copies, waits for them, and re-layouts  2.87 us

profile of v3, /device:TPU:32, one launch (start us, length us, event | category | flops | bytes accessed | tf_op | source)
XLA Modules:
  0.0 111.2 jit_solution(1007642299194651980)
XLA Ops:
  0.6 1.3 %bitcast_convert_fusion.outw = f32[26,128]{1,0:T(8,128)} fusion(bf16[3328]{0:T(1024)(128)(2,1)} %param.17), kind=kLoop, calls=%fused_computation.1 | loop fusion | flops 3328 | bytes 19968 | tf_op jit(solution)/shard_map/reshape | solution.py:587
  1.9 0.7 reshape.33
  2.6 0.6 pad.4.reqs
  3.2 102.5 %shard_map.136 = (f32[2048,128]{1,0:T(8,128)}, f32[16,128]{1,0:T(8,128)}, f32[16,512]{1,0:T(8,128)}, f32[8,128]{1,0:T(8,128)}) custom-call(f32[2048,128]{1,0:T(8,128)} %table_in.1, f32[16,128]{1,0:T(8,128)} %bitcast.20, s32[16,128]{1,0:T(8,128)} %pad.4.reqs, s32[3,104,128]{2,1,0:T(8,128)} %bitcast.18, s32[3,128]{1,0:T(4,128)} %labels.1, ...), custom_call_target="tpu_custom_call" | custom-call | tf_op jit(solution)/shard_map/pallas_call | solution.py:571
  105.7 0.0 copy-start
  105.7 1.4 %slice_bitcast_fusion = (f32[256,13]{0,1:T(8,128)}, f32[13,256]{1,0:T(8,128)}) fusion(f32[16,512]{1,0:T(8,128)} %get-tuple-element.12), kind=kLoop, calls=%fused_computation | loop fusion | bytes 53248 | tf_op jit(solution)/shard_map/transpose | solution.py:593
  107.1 1.3 %slice_bitcast_fusion.1 = (f32[13]{0:T(128)}, f32[13]{0:T(128)}) fusion(f32[8,128]{1,0:T(8,128)} %get-tuple-element.13), kind=kLoop, calls=%fused_computation.2 | loop fusion | bytes 208 | tf_op jit(solution)/shard_map/squeeze | solution.py:595
  108.4 2.3 %copy.17 = f32[2048,128]{1,0:T(8,128)} copy(f32[2048,128]{1,0:T(8,128)} %get-tuple-element.24) | data formatting | bytes 2097152
  110.6 0.0 copy-done
  110.6 0.6 copy.18
Async XLA Ops:
  105.7 4.9 %copy-start = (f32[16,128]{1,0:T(8,128)S(1)}, f32[16,128]{1,0:T(8,128)}, u32[]{:S(2)}) copy-start(f32[16,128]{1,0:T(8,128)} %get-tuple-element.11) | copy-start | bytes 24580

commit v4 on v3

--- a/solution.py
+++ b/solution.py
@@ -23,7 +23,8 @@
 NCH = D_IN // CH
 NROW = ROWS // CH
 UNROLL = 13
-UNROLL_ROWS = 4
+ORDER = (2, 1, 3, 0)
+UNROLL_ROWS = 8
 XROWS = D_IN // NX
 BLOCK = XROWS // NZ
 HALF = BLOCK // NC
@@ -75,9 +76,9 @@
     table_hbm, accum_out, gdu_out, bo_out,
     table, mem, down, up,
     rqs, rqr, wcol, wrow, s1, r1, g1, g2, rr, rt,
-    down_t, up_t, bias_b, out_b, acc_b, posq,
-    counts, x0s, dgs, lows, dlows, gates, x1s, bo3,
-    xw, xo, dw, do, lowp, dlowp, sa, ra, sb, rb, a2, ra2, b2, rb2, z3, rz,
+    rpad, outf, both_t, up_t, bias_b, out_b, acc_b, posq,
+    counts, x0s, glows, dlows, us, x1s, heads,
+    xw, xo, glowp, dlowp, sa, ra, sb, rb, a2, ra2, b2, rb2, z3, rz,
     bo, boc, bw, bwx, bv, bvy, bvz,
     lsem, qs, qr, s1s, s1r, g1s, g1r,
     fs, fr, xs, xr, ys, yr, x2s, x2r, y2s, y2r, zs, zr,
@@ -137,13 +138,18 @@
             device_id=partner, device_id_type=pl.DeviceIdType.MESH,
         )
 
-    flat = jnp.concatenate([reqs[...].astype(F32), jnp.zeros((E - 16, E), F32)], axis=0).T
+    rpad[...] = jnp.zeros_like(rpad)
+    for t in range(STEPS):
+        rpad[t * SLOTS:(t + 1) * SLOTS, 0:OWNERS] = reqs[t].astype(F32)
+    flat = rpad[...].T
     rqs[:, 0, :] = flat[0:OWNERS]
+    outf[...] = outw[...].astype(F32)
+    out_b[D_IN:, :] = jnp.zeros((16, E), F32)
 
     def columns(i, carry):
         at = al(i * E, E)
         bias_b[pl.ds(at, E), :] = jnp.broadcast_to(bias[pl.ds(i, 1), :], (E, E)).T
-        out_b[pl.ds(at, E), :] = jnp.broadcast_to(outw[pl.ds(i, 1), :], (E, E)).T
+        out_b[pl.ds(at, E), :] = jnp.broadcast_to(outf[pl.ds(i, 1), :], (E, E)).T
         return carry
 
     lax.fori_loop(0, NB, columns, 0, unroll=2)
@@ -177,8 +183,11 @@
 
     def weights(i, carry):
         at = al(i * CH, CH)
-        down_t[:, pl.ds(at, CH)] = nt(eye, down[pl.ds(at, CH), :]).astype(BF16)
-        up_t[pl.ds(at, CH), :] = nt(eye, up[:, pl.ds(at, CH)]).astype(BF16)
+        both_t[0:RANK, pl.ds(at, CH)] = nt(eye, down[pl.ds(at, CH), :]).astype(BF16)
+        up_c = up[:, pl.ds(at, CH)]
+        up_t[pl.ds(at, CH), :] = nt(eye, up_c).astype(BF16)
+        w_row = jnp.concatenate([outf[pl.ds(2 * i, 1), :], outf[pl.ds(2 * i + 1, 1), :]], axis=1)
+        both_t[RANK:, pl.ds(at, CH)] = (up_c.astype(F32) * w_row).astype(BF16)
         return carry
 
     lax.fori_loop(0, NCH, weights, 0)
@@ -189,7 +198,6 @@
         return carry
 
     lax.fori_loop(0, ROWS // E, acc_columns, 0, unroll=2)
-    bo3[...] = jnp.zeros_like(bo3)
     loads[2].wait()
     count(0)
 
@@ -240,10 +248,17 @@
             device_id=peer, device_id_type=pl.DeviceIdType.MESH,
         )
 
+    def rows_copy(t):
+        return copy_to(xo.at[t], xw.at[t, 1], fs.at[t, 0], fr.at[t, 0], partner)
+
+    def glow_copy(t):
+        return copy_to(glows.at[t], glowp.at[t], fs.at[t, 1], fr.at[t, 1], partner)
+
+    def dlow_copy(t):
+        return copy_to(dlows.at[t], dlowp.at[t], fs.at[t, 2], fr.at[t, 2], partner)
+
     def factors(t):
-        pairs = ((xo.at[t], xw.at[t, 1]), (do.at[t], dw.at[t, 1]),
-                 (lows.at[t], lowp.at[t]), (dlows.at[t], dlowp.at[t]))
-        return [copy_to(a, b, fs.at[t, n], fr.at[t, n], partner) for n, (a, b) in enumerate(pairs)]
+        return [rows_copy(t), glow_copy(t), dlow_copy(t)]
 
     def windows(t):
         def one(i, carry):
@@ -252,13 +267,10 @@
             other = pl.ds(al((i * BLOCK + HALF * (1 - c)) // 16 * 16, 16), GROUP)
             xw[t, 0, to, :] = x0s[t, mine, :]
             xo[t, to, :] = x0s[t, other, :]
-            dw[t, 0, to, :] = dgs[t, mine, :]
-            do[t, to, :] = dgs[t, other, :]
             return carry
 
         lax.fori_loop(0, NX * NZ, one, 0, unroll=4)
-        for copy in factors(t):
-            copy.start()
+        rows_copy(t).start()
 
     mi = iota((CH, CH), 0)
     m_in = lax.rem(mi, 16)
@@ -267,7 +279,7 @@
     spots = onehot((m_col == iota((CH, CH), 1)) & (m_in < SHARE))
 
     def stage_x(k):
-        return copy_to(sa.at[k - 1], ra.at[k - 1], xs.at[k], xr.at[k], xpeer(k)[1])
+        return copy_to(sa.at[k], ra.at[k - 1], xs.at[k], xr.at[k], xpeer(k)[1])
 
     def stage_y(i, k):
         py, d = ypeer(k)
@@ -278,7 +290,7 @@
         return copy_to(a2.at[py], ra2.at[k - 1], y2s.at[k], y2r.at[k], d)
 
     def stage_x2(k):
-        return copy_to(b2.at[k - 1], rb2.at[k - 1], x2s.at[k], x2r.at[k], xpeer(k)[1])
+        return copy_to(b2.at[k], rb2.at[k - 1], x2s.at[k], x2r.at[k], xpeer(k)[1])
 
     def stage_z(k):
         pz, d = zpeer(k)
@@ -298,39 +310,44 @@
         return copy_to(bv.at[1], bvz.at[k - 1], bzs.at[k], bzr.at[k], zpeer(k)[1])
 
     def dense():
-        windows(STEPS - 1)
-        bo[...] = jnp.zeros_like(bo)
-        for i in range(NCH):
-            b_row = bo3[0, i][3:4, :]
-            o_rows = bo3[1, i]
-            o_row = o_rows[0:1, :] + o_rows[1:2, :] + o_rows[2:3, :]
-            for h in range(2):
-                bo[0, 2 * i + h:2 * i + h + 1, :] = b_row[:, h * E:(h + 1) * E]
-                bo[0, 32 + 2 * i + h:33 + 2 * i + h, :] = o_row[:, h * E:(h + 1) * E]
-        bo_core().start()
         for t in range(STEPS):
             for copy in factors(t):
                 copy.wait_recv()
-        dl = jnp.concatenate([r[t] for t in range(STEPS) for r in (dlows, dlowp)], axis=1)
-        lo = jnp.concatenate([r[t] for t in range(STEPS) for r in (lows, lowp)], axis=1)
+        right = jnp.concatenate([
+            jnp.concatenate([r[t] for t in range(STEPS) for r in (dlows, dlowp)], axis=1),
+            jnp.concatenate([r[t] for t in range(STEPS) for r in (glows, glowp)], axis=1),
+        ], axis=0)
         for i in range(NX):
-            px = at_x[(i + 1) % NX]
+            px = at_x[ORDER[i]]
             for h in range(2):
                 rows = pl.ds(al((px * 2 + h) * CH, CH), CH)
                 xx = jnp.concatenate([xw[t, p, rows, :] for t in range(STEPS) for p in range(2)], axis=1)
-                dd = jnp.concatenate([dw[t, p, rows, :] for t in range(STEPS) for p in range(2)], axis=1)
-                g = jnp.concatenate([nt(xx, dl).astype(BF16), nt(dd, lo).astype(BF16)], axis=1)
-                g = nn(spots, g).astype(BF16)
+                g = nn(spots, nt(xx, right).astype(BF16)).astype(BF16)
                 for zl in range(NZ // 2):
                     to = (h * (NZ // 2) + zl) * 16
                     for py in range(NY):
                         at = (zl * NY + py) * 16
-                        sa[i, py, to:to + 16, :] = g[at:at + 16, :RANK]
-                        sb[py, i, to:to + 16, :] = g[at:at + 16, RANK:]
-            if i < NX - 1:
-                stage_x(i + 1).start()
-            for k in range(1, NY):
-                stage_y(i, k).start()
+                        sa[ORDER[i], py, to:to + 16, :] = g[at:at + 16, :RANK]
+                        sb[py, ORDER[i], to:to + 16, :] = g[at:at + 16, RANK:]
+            if ORDER[i]:
+                stage_x(ORDER[i]).start()
+            for k in (2, 1, 3):
+                stage_y(ORDER[i], k).start()
+
+    def sums():
+        head = jnp.concatenate([heads[t] for t in range(STEPS)], axis=1)
+        bo[...] = jnp.zeros_like(bo)
+        for i in range(NCH):
+            at = i * CH
+            b_rows = nt(head, jnp.concatenate([x0s[t, at:at + CH, :] for t in range(STEPS)], axis=1))
+            o_rows = nt(head, jnp.concatenate([x1s[t, at:at + CH, :] for t in range(STEPS)], axis=1))
+            b_row = b_rows[0:1, :] + b_rows[1:2, :] + b_rows[2:3, :]
+            o_row = o_rows[0:1, :] + o_rows[1:2, :] + o_rows[2:3, :]
+            for h in range(2):
+                k = 2 * i + h
+                bo[0, k:k + 1, :] = b_row[:, h * E:(h + 1) * E] * outf[k:k + 1, :]
+                bo[0, 32 + k:33 + k, :] = o_row[:, h * E:(h + 1) * E]
+        bo_core().start()
         bo_core().wait()
         both = bo[0] + boc[...]
         bo[1] = both
@@ -351,20 +368,20 @@
             stage_x(k).wait()
         for py in range(NY):
             a2[py] = (
-                sa[NX - 1, py].astype(F32)
+                sa[0, py].astype(F32)
                 + ra[0, py].astype(F32) + ra[1, py].astype(F32) + ra[2, py].astype(F32)
             ).astype(BF16)
         for k in range(1, NY):
             stage_y2(k).start()
-        for i in range(NX):
+        for i in ORDER:
             for k in range(1, NY):
                 stage_y(i, k).wait()
             b2[i] = (
                 sb[y, i].astype(F32)
                 + rb[0, i].astype(F32) + rb[1, i].astype(F32) + rb[2, i].astype(F32)
             ).astype(BF16)
-            if i < NX - 1:
-                stage_x2(i + 1).start()
+            if i:
+                stage_x2(i).start()
 
     def step(t, carry):
         send_all(s1.at[t], r1.at[t], s1s.at[t], s1r.at[t])
@@ -375,25 +392,36 @@
         sent_all(s1.at[t], r1.at[t], s1s.at[t], s1r.at[t]).wait_recv()
         fetched_t = nt(eye_e, take(r1, t).astype(BF16)).astype(BF16)
 
-        def pool(i, low):
+        def pool(i, carry):
             xx = nn(fetched_t, counts[cur, i]).astype(BF16)
-            xx = jnp.concatenate([xx[:, :TOK], xx[:, TOK:]], axis=0)
             at = al(i * CH, CH)
-            x0s[t, pl.ds(at, CH), :] = xx
-            return low + nn(down_t[:, pl.ds(at, CH)], xx)
-
-        low = lax.fori_loop(0, NCH, pool, jnp.zeros((RANK, TOK), F32), unroll=UNROLL).astype(BF16)
-        lows[t] = low
+            x0s[t, pl.ds(at, E), :] = xx[:, :TOK]
+            x0s[t, pl.ds(al(at + E, E), E), :] = xx[:, TOK:]
+            return carry
+
+        def project(i, total):
+            at = al(i * CH, CH)
+            return total + nn(both_t[:, pl.ds(at, CH)], x0s[t, pl.ds(at, CH), :])
+
+        lax.fori_loop(0, NCH, pool, 0, unroll=UNROLL)
+        total = lax.fori_loop(0, NCH, project, jnp.zeros((2 * RANK, TOK), F32), unroll=UNROLL)
+        low = total[:RANK].astype(BF16)
+        v = total[RANK:]
+        vb = v.astype(BF16)
+
+        @pl.when(t == STEPS - 1)
+        def _():
+            windows(t)
 
         def forward(i, logit):
             at = al(i * CH, CH)
             gate = nn(up_t[pl.ds(at, CH), :], low) + bias_b[pl.ds(at, CH), :]
-            gates[pl.ds(at, CH), :] = gate
             x0f = x0s[t, pl.ds(at, CH), :].astype(F32)
+            w = out_b[pl.ds(at, CH), :]
+            us[pl.ds(at, CH), :] = w * (gate + 1.0) + nn(down[pl.ds(at, CH), :], vb)
             x1 = (x0f * gate + x0f).astype(BF16)
-            x1s[pl.ds(at, CH), :] = x1
-            prod = x1.astype(F32) * out_b[pl.ds(at, CH), :]
-            return logit + jnp.sum(prod.reshape(CH // 8, 8, TOK), axis=0)
+            x1s[t, pl.ds(at, CH), :] = x1
+            return logit + jnp.sum((x1.astype(F32) * w).reshape(CH // 8, 8, TOK), axis=0)
 
         logit = lax.fori_loop(0, NCH, forward, jnp.zeros((8, TOK), F32), unroll=UNROLL)
         logit = jnp.sum(logit, axis=0, keepdims=True)
@@ -402,20 +430,12 @@
         dmid = (dlogit - dhi).astype(BF16).astype(F32)
         dlo = dlogit - dhi - dmid
         sub = iota((16, TOK), 0)
-        heads = jnp.where(sub == 0, dhi, jnp.where(sub == 1, dmid, jnp.where(sub == 2, dlo, 1.0)))
-        heads = heads.astype(BF16)
-
-        def backward(i, dlow):
-            at = al(i * CH, CH)
-            x0f = x0s[t, pl.ds(at, CH), :].astype(F32)
-            dg = (dlogit * out_b[pl.ds(at, CH), :] * x0f).astype(BF16)
-            dgs[t, pl.ds(at, CH), :] = dg
-            bo3[0, i] = bo3[0, i] + nt(heads, dg)
-            bo3[1, i] = bo3[1, i] + nt(heads, x1s[pl.ds(at, CH), :])
-            return dlow + nn(up[:, pl.ds(at, CH)], dg)
-
-        dlow = lax.fori_loop(0, NCH, backward, jnp.zeros((RANK, TOK), F32), unroll=UNROLL).astype(BF16)
-        dlows[t] = dlow
+        split = jnp.where(sub == 0, dhi, jnp.where(sub == 1, dmid, jnp.where(sub == 2, dlo, 0.0)))
+        heads[t] = split.astype(BF16)
+        dlows[t] = (dlogit * v).astype(BF16)
+        glows[t] = (dlogit * low.astype(F32)).astype(BF16)
+        dlow_copy(t).start()
+        glow_copy(t).start()
 
         @pl.when(t == STEPS - 1)
         def _():
@@ -423,8 +443,7 @@
 
         def spread(i, gf):
             at = al(i * CH, CH)
-            dx0 = dlogit * out_b[pl.ds(at, CH), :] * (gates[pl.ds(at, CH), :] + 1.0)
-            dx0 = (dx0 + nn(down[pl.ds(at, CH), :], dlow)).astype(BF16)
+            dx0 = (dlogit * us[pl.ds(at, CH), :]).astype(BF16)
             both = jnp.concatenate([dx0[:E], dx0[E:]], axis=1)
             return gf + nt(counts[cur, i], both)
 
@@ -439,6 +458,7 @@
 
         @pl.when(t == STEPS - 1)
         def _():
+            sums()
             second()
 
         sent_all(g1.at[t], g2.at[t], g1s.at[t], g1r.at[t]).wait_recv()
@@ -446,17 +466,20 @@
         hi = back.astype(BF16)
         pair = jnp.concatenate([hi, (back - hi.astype(F32)).astype(BF16)], axis=1)
 
-        def update(j, rows):
+        def update(j, carry):
             at = al(j * CH, CH)
             rg = nn(rt[j], pair)
             rg = rg[:, :E] + rg[:, E:]
             acc = acc_b[pl.ds(at, CH), :] + jnp.mean(rg * rg, axis=1, keepdims=True)
             acc_b[pl.ds(at, CH), :] = acc
-            new = table[pl.ds(at, CH), :] - learn_rate * rg * lax.rsqrt(acc)
-            table[pl.ds(at, CH), :] = new
-            return rows + nn(rr[j], new.astype(BF16))
-
-        rows = lax.fori_loop(0, NROW, update, jnp.zeros((FETCH, E), F32), unroll=UNROLL_ROWS)
+            table[pl.ds(at, CH), :] = table[pl.ds(at, CH), :] - learn_rate * rg * lax.rsqrt(acc)
+            return carry
+
+        def gather(j, rows):
+            return rows + nn(rr[j], table[pl.ds(al(j * CH, CH), CH), :].astype(BF16))
+
+        lax.fori_loop(0, NROW, update, 0, unroll=UNROLL_ROWS)
+        rows = lax.fori_loop(0, NROW, gather, jnp.zeros((FETCH, E), F32), unroll=NROW)
         put(s1, t + 1, rows)
         return carry
 
@@ -485,7 +508,7 @@
         a2[y].astype(F32) + ra2[0].astype(F32) + ra2[1].astype(F32) + ra2[2].astype(F32)
     ).astype(BF16)
     z3[:, RANK:] = (
-        b2[NX - 1].astype(F32) + rb2[0].astype(F32) + rb2[1].astype(F32) + rb2[2].astype(F32)
+        b2[0].astype(F32) + rb2[0].astype(F32) + rb2[1].astype(F32) + rb2[2].astype(F32)
     ).astype(BF16)
     for k in range(1, NZ):
         stage_z(k).start()
@@ -511,7 +534,10 @@
     total = z3[pl.ds(al(z * 16, 16), 16), :].astype(F32)
     for k in range(NZ - 1):
         total = total + rz[k].astype(F32)
-    gdu_out[...] = total * scale
+    own = owner * NY + y
+    w = out_b[pl.ds(own * SHARE, 16), :]
+    gdu_out[:, :RANK] = total[:, :RANK] * scale
+    gdu_out[:, RANK:] = total[:, RANK:] * scale * jnp.concatenate([w, w], axis=1)
 
     for t in range(STEPS):
         for copy in factors(t):
@@ -523,9 +549,25 @@
     store.wait()
 
 
+def finish(table_in, accum_in, gdu, bo, table, accum, down, up, bias, outw, sem):
+    rows = ROWS // 8
+    copies = [
+        pltpu.make_async_copy(table_in.at[pl.ds(n * rows, rows)], table.at[pl.ds(n * rows, rows)], sem.at[n])
+        for n in range(8)
+    ]
+    for copy in copies:
+        copy.start()
+    accum[...] = accum_in[...]
+    down[...] = gdu[0:SHARE, :RANK]
+    up[...] = gdu[0:SHARE, RANK:]
+    bias[...] = bo[0:1, 0:SHARE]
+    outw[...] = bo[1:2, 0:SHARE]
+    for copy in copies:
+        copy.wait()
+
+
 def local(table, accum, requests, members, labels, down_proj, up_proj, cross_bias, out_weight):
-    reqs = jnp.transpose(requests[:, 0, 0], (0, 2, 1)).reshape(STEPS * SLOTS, OWNERS)
-    reqs = jnp.pad(reqs, ((0, 4), (0, E - OWNERS)))
+    reqs = jnp.transpose(requests[:, 0, 0], (0, 2, 1))
     mem = jnp.transpose(members, (0, 2, 3, 1)).reshape(STEPS, NB * BAGLEN, TOK)
     dma = pltpu.SemaphoreType.DMA
     vm = pltpu.VMEM
@@ -539,13 +581,12 @@
     scratch += [vm((STEPS, OWNERS, SLOTS, E), F32)] * 3
     scratch += [
         vm((NROW, FETCH, CH), BF16), vm((NROW, CH, FETCH), BF16),
-        vm((RANK, D_IN), BF16), vm((D_IN, RANK), BF16),
-        vm((D_IN, TOK), F32), vm((D_IN, TOK), F32), vm((ROWS, E), F32), vm((FETCH, E), jnp.int32),
+        vm((E, E), F32), vm((NB, E), F32), vm((2 * RANK, D_IN), BF16), vm((D_IN, RANK), BF16),
+        vm((D_IN, TOK), F32), vm((D_IN + 16, TOK), F32), vm((ROWS, E), F32), vm((FETCH, E), jnp.int32),
         vm((2, NCH, FETCH, 2 * TOK), BF16),
-        vm((STEPS, D_IN, TOK), BF16), vm((STEPS, D_IN, TOK), BF16),
+        vm((STEPS, D_IN, TOK), BF16),
         vm((STEPS, RANK, TOK), BF16), vm((STEPS, RANK, TOK), BF16),
-        vm((D_IN, TOK), F32), vm((D_IN, TOK), BF16), vm((2, NCH, 16, CH), F32),
-        vm((STEPS, 2, CORE_ROWS, TOK), BF16), vm((STEPS, CORE_ROWS, TOK), BF16),
+        vm((D_IN, TOK), F32), vm((STEPS, D_IN, TOK), BF16), vm((STEPS, 16, TOK), BF16),
         vm((STEPS, 2, CORE_ROWS, TOK), BF16), vm((STEPS, CORE_ROWS, TOK), BF16),
         vm((STEPS, RANK, TOK), BF16), vm((STEPS, RANK, TOK), BF16),
         vm((NX, NY, NZ * 16, RANK), BF16), vm((NX - 1, NY, NZ * 16, RANK), BF16),
@@ -584,16 +625,23 @@
         ),
     )(
         table, accum.reshape(ROWS // E, E), reqs, mem, labels, down_proj, up_proj,
-        cross_bias.reshape(NB, E), out_weight.astype(F32).reshape(NB, E),
+        cross_bias.reshape(NB, E), out_weight.reshape(NB, E),
     )
-    return (
-        table_new,
-        accum_new.reshape(ROWS),
-        gdu[:SHARE, :RANK],
-        gdu[:SHARE, RANK:].T,
-        bo[0, :SHARE],
-        bo[1, :SHARE],
-    )
+    table_out, accum_out, down, up, bias, outw = pl.pallas_call(
+        finish,
+        out_shape=(
+            jax.ShapeDtypeStruct((ROWS, E), F32),
+            jax.ShapeDtypeStruct((ROWS // E, E), F32),
+            jax.ShapeDtypeStruct((SHARE, RANK), F32),
+            jax.ShapeDtypeStruct((SHARE, RANK), F32),
+            jax.ShapeDtypeStruct((1, SHARE), F32),
+            jax.ShapeDtypeStruct((1, SHARE), F32),
+        ),
+        in_specs=[hbm, spec, spec, spec],
+        out_specs=(spec, spec, spec, spec, spec, spec),
+        scratch_shapes=[dma((8,))],
+    )(table_new, accum_new, gdu, bo)
+    return (table_out, accum_out.reshape(ROWS), down, up.T, bias[0], outw[0])
 
 
 def solution(mesh):

time: 113 us -> 103 us (0.912); the launches traced: 111 us -> 103 us
  local copies, waits for them, and re-layouts: 6.79 us -> 0 us
  other arithmetic: 1.3 us -> 0 us
    pallas_call x1, Pallas kernels: 102 us -> 98.8 us  [local(): pl.pallas_call(kernel, out_shape=(jax.ShapeDtypeStruct((ROWS, E), F32), j...]
    pallas_call x0 -> x1, Pallas kernels: none -> 3.1 us  [local(): pl.pallas_call(finish, out_shape=(jax.ShapeDtypeStruct((ROWS, E), F32), j...]
    unnamed x4 -> x0, local copies, waits for them, and re-layouts: 2.87 us -> none
    transpose x1 -> x0, local copies, waits for them, and re-layouts: 1.35 us -> none  [local(): gdu[:SHARE, RANK:]]
    reshape x1 -> x0, other arithmetic: 1.3 us -> none  [local(): out_weight.astype(F32).reshape(NB, E)]
    squeeze x1 -> x0, local copies, waits for them, and re-layouts: 1.27 us -> none  [local(): bo[1, :SHARE]]
where the time goes in v4:
time: 103 us
  Pallas kernels  102 us (99%)
    pallas_call x1, Pallas kernels, local(): pl.pallas_call(kernel, out_shape=(jax.ShapeDtypeStruct((ROWS, E), F32), j...  98.8 us
    pallas_call x1, Pallas kernels, local(): pl.pallas_call(finish, out_shape=(jax.ShapeDtypeStruct((ROWS, E), F32), j...  3.1 us

profile of v4, /device:TPU:32, one launch (start us, length us, event | category | flops | bytes accessed | tf_op | source)
XLA Modules:
  0.0 102.6 jit_solution(972512446123634909)
XLA Ops:
  0.6 98.8 %shard_map.136 = (f32[2048,128]{1,0:T(8,128)}, f32[16,128]{1,0:T(8,128)}, f32[16,512]{1,0:T(8,128)}, f32[8,128]{1,0:T(8,128)}) custom-call(f32[2048,128]{1,0:T(8,128)} %table_in.1, f32[16,128]{1,0:T(8,128)} %bitcast.15, s32[3,4,64]{2,1,0:T(4,128)} %bitcast.17, s32[3,104,128]{2,1,0:T(8,128)} %bitcast.13, s32[3,128]{1,0:T(4,128)} %labels.1, ...), custom_call_target="tpu_custom_call" | custom-call | tf_op jit(solution)/shard_map/pallas_call | solution.py:612
  99.5 3.1 %shard_map.137 = (f32[2048,128]{1,0:T(8,128)}, f32[16,128]{1,0:T(8,128)}, f32[13,256]{1,0:T(8,128)}, f32[13,256]{1,0:T(8,128)}, f32[1,13]{1,0:T(1,128)}, /*index=5*/f32[1,13]{1,0:T(1,128)}) custom-call(f32[2048,128]{1,0:T(8,128)} %get-tuple-element.16.table_in, f32[16,128]{1,0:T(8,128)} %get-tuple-element.17.accum_in, f32[16,512]{1,0:T(8,128)} %get-tuple-element.18.gdu, ...), custom_call_target="tpu_custom_call" | custom-call | tf_op jit(solution)/shard_map/pallas_call | solution.py:630

commit v5 on v4

--- a/solution.py
+++ b/solution.py
@@ -278,23 +278,33 @@
     m_col = mi // GROUP * GROUP + m_off + lax.rem(mi // 16, NY) * SHARE + m_in
     spots = onehot((m_col == iota((CH, CH), 1)) & (m_in < SHARE))
 
-    def stage_x(k):
-        return copy_to(sa.at[k], ra.at[k - 1], xs.at[k], xr.at[k], xpeer(k)[1])
-
-    def stage_y(i, k):
+    def cut(h):
+        return pl.ds(h * (NZ // 2) * 16, (NZ // 2) * 16)
+
+    def stage_x(k, h):
+        return copy_to(
+            sa.at[k, :, cut(h)], ra.at[k - 1, :, cut(h)], xs.at[k, h], xr.at[k, h], xpeer(k)[1]
+        )
+
+    def stage_y(i, k, h):
         py, d = ypeer(k)
-        return copy_to(sb.at[py, i], rb.at[k - 1, i], ys.at[i, k], yr.at[i, k], d)
-
-    def stage_y2(k):
+        return copy_to(
+            sb.at[py, i, cut(h)], rb.at[k - 1, i, cut(h)], ys.at[i, k, h], yr.at[i, k, h], d
+        )
+
+    def stage_y2(k, h):
         py, d = ypeer(k)
-        return copy_to(a2.at[py], ra2.at[k - 1], y2s.at[k], y2r.at[k], d)
-
-    def stage_x2(k):
-        return copy_to(b2.at[k], rb2.at[k - 1], x2s.at[k], x2r.at[k], xpeer(k)[1])
-
-    def stage_z(k):
-        pz, d = zpeer(k)
-        return copy_to(z3.at[pl.ds(al(pz * 16, 16), 16)], rz.at[k - 1], zs.at[k], zr.at[k], d)
+        return copy_to(a2.at[py, cut(h)], ra2.at[k - 1, cut(h)], y2s.at[k, h], y2r.at[k, h], d)
+
+    def stage_x2(k, h):
+        return copy_to(
+            b2.at[k, cut(h)], rb2.at[k - 1, cut(h)], x2s.at[k, h], x2r.at[k, h], xpeer(k)[1]
+        )
+
+    def z_copy(k, zt):
+        return copy_to(
+            z3.at[pl.ds(al(zt * 16, 16), 16)], rz.at[z], zs.at[k], zr.at[z], dev(x, zt, c, y)
+        )
 
     def bo_core():
         return copy_to(bo.at[0], boc, bcs, bcr, partner)
@@ -317,9 +327,9 @@
             jnp.concatenate([r[t] for t in range(STEPS) for r in (dlows, dlowp)], axis=1),
             jnp.concatenate([r[t] for t in range(STEPS) for r in (glows, glowp)], axis=1),
         ], axis=0)
-        for i in range(NX):
-            px = at_x[ORDER[i]]
-            for h in range(2):
+        for h in range(2):
+            for i in range(NX):
+                px = at_x[ORDER[i]]
                 rows = pl.ds(al((px * 2 + h) * CH, CH), CH)
                 xx = jnp.concatenate([xw[t, p, rows, :] for t in range(STEPS) for p in range(2)], axis=1)
                 g = nn(spots, nt(xx, right).astype(BF16)).astype(BF16)
@@ -329,10 +339,10 @@
                         at = (zl * NY + py) * 16
                         sa[ORDER[i], py, to:to + 16, :] = g[at:at + 16, :RANK]
                         sb[py, ORDER[i], to:to + 16, :] = g[at:at + 16, RANK:]
-            if ORDER[i]:
-                stage_x(ORDER[i]).start()
-            for k in (2, 1, 3):
-                stage_y(ORDER[i], k).start()
+                if ORDER[i]:
+                    stage_x(ORDER[i], h).start()
+                for k in (2, 1, 3):
+                    stage_y(ORDER[i], k, h).start()
 
     def sums():
         head = jnp.concatenate([heads[t] for t in range(STEPS)], axis=1)
@@ -364,24 +374,54 @@
         bv[0] = bw[x] + bwx[0] + bwx[1] + bwx[2]
         for k in range(1, NY):
             bo_y(k).start()
+        first(0)
+        first(1)
+
+    def first(h):
         for k in range(1, NX):
-            stage_x(k).wait()
+            stage_x(k, h).wait()
         for py in range(NY):
-            a2[py] = (
-                sa[0, py].astype(F32)
-                + ra[0, py].astype(F32) + ra[1, py].astype(F32) + ra[2, py].astype(F32)
+            a2[py, cut(h)] = (
+                sa[0, py, cut(h)].astype(F32)
+                + ra[0, py, cut(h)].astype(F32) + ra[1, py, cut(h)].astype(F32)
+                + ra[2, py, cut(h)].astype(F32)
             ).astype(BF16)
-        for k in range(1, NY):
-            stage_y2(k).start()
+        for k in (2, 1, 3):
+            stage_y2(k, h).start()
         for i in ORDER:
             for k in range(1, NY):
-                stage_y(i, k).wait()
-            b2[i] = (
-                sb[y, i].astype(F32)
-                + rb[0, i].astype(F32) + rb[1, i].astype(F32) + rb[2, i].astype(F32)
+                stage_y(i, k, h).wait()
+            b2[i, cut(h)] = (
+                sb[y, i, cut(h)].astype(F32)
+                + rb[0, i, cut(h)].astype(F32) + rb[1, i, cut(h)].astype(F32)
+                + rb[2, i, cut(h)].astype(F32)
             ).astype(BF16)
             if i:
-                stage_x2(i).start()
+                stage_x2(i, h).start()
+
+    def third(h):
+        for k in range(1, NY):
+            stage_y2(k, h).wait()
+        for k in range(1, NX):
+            stage_x2(k, h).wait()
+        z3[cut(h), :RANK] = (
+            a2[y, cut(h)].astype(F32) + ra2[0, cut(h)].astype(F32) + ra2[1, cut(h)].astype(F32)
+            + ra2[2, cut(h)].astype(F32)
+        ).astype(BF16)
+        z3[cut(h), RANK:] = (
+            b2[0, cut(h)].astype(F32) + rb2[0, cut(h)].astype(F32) + rb2[1, cut(h)].astype(F32)
+            + rb2[2, cut(h)].astype(F32)
+        ).astype(BF16)
+        for k in range(NZ // 2):
+            zt = h * (NZ // 2) + k
+
+            @pl.when(zt != z)
+            def _():
+                z_copy(zt, zt).start()
+
+            @pl.when(zt == z)
+            def _():
+                rz[z] = z3[zt * 16:zt * 16 + 16, :]
 
     def step(t, carry):
         send_all(s1.at[t], r1.at[t], s1s.at[t], s1r.at[t])
@@ -437,10 +477,6 @@
         dlow_copy(t).start()
         glow_copy(t).start()
 
-        @pl.when(t == STEPS - 1)
-        def _():
-            dense()
-
         def spread(i, gf):
             at = al(i * CH, CH)
             dx0 = (dlogit * us[pl.ds(at, CH), :]).astype(BF16)
@@ -458,8 +494,8 @@
 
         @pl.when(t == STEPS - 1)
         def _():
+            dense()
             sums()
-            second()
 
         sent_all(g1.at[t], g2.at[t], g1s.at[t], g1r.at[t]).wait_recv()
         back = take(g2, t)
@@ -495,23 +531,14 @@
 
     lax.fori_loop(0, ROWS // E, acc_rows, 0)
 
+    second()
     for k in range(1, NY):
         bo_y(k).wait()
     bv[1] = bv[0] + bvy[0] + bvy[1] + bvy[2]
     for k in range(1, NZ):
         bo_z(k).start()
-    for k in range(1, NY):
-        stage_y2(k).wait()
-    for k in range(1, NX):
-        stage_x2(k).wait()
-    z3[:, :RANK] = (
-        a2[y].astype(F32) + ra2[0].astype(F32) + ra2[1].astype(F32) + ra2[2].astype(F32)
-    ).astype(BF16)
-    z3[:, RANK:] = (
-        b2[0].astype(F32) + rb2[0].astype(F32) + rb2[1].astype(F32) + rb2[2].astype(F32)
-    ).astype(BF16)
-    for k in range(1, NZ):
-        stage_z(k).start()
+    third(0)
+    third(1)
 
     scale = 1.0 / (STEPS * TOK * NX * NY * NZ * NC)
     for k in range(1, NZ):
@@ -529,10 +556,13 @@
         rows.append(pltpu.roll(pair, lax.rem(2 * E - lax.rem(start, E), 2 * E), 1)[:, 0:E])
     bo_out[...] = jnp.where(iota((8, E), 0) == 0, rows[0], rows[1])
 
+    for k in range(NZ):
+        @pl.when(k != z)
+        def _():
+            copy_to(z3.at[pl.ds(0, 16)], rz.at[k], zs.at[0], zr.at[k], partner).wait_recv()
+            z_copy(k, k).wait_send()
+    total = rz[0].astype(F32)
     for k in range(1, NZ):
-        stage_z(k).wait()
-    total = z3[pl.ds(al(z * 16, 16), 16), :].astype(F32)
-    for k in range(NZ - 1):
         total = total + rz[k].astype(F32)
     own = owner * NY + y
     w = out_b[pl.ds(own * SHARE, 16), :]
@@ -593,7 +623,7 @@
         vm((NY, NX, NZ * 16, RANK), BF16), vm((NY - 1, NX, NZ * 16, RANK), BF16),
         vm((NY, NZ * 16, RANK), BF16), vm((NY - 1, NZ * 16, RANK), BF16),
         vm((NX, NZ * 16, RANK), BF16), vm((NX - 1, NZ * 16, RANK), BF16),
-        vm((NZ * 16, 2 * RANK), BF16), vm((NZ - 1, 16, 2 * RANK), BF16),
+        vm((NZ * 16, 2 * RANK), BF16), vm((NZ, 16, 2 * RANK), BF16),
         vm((2, 64, E), F32), vm((64, E), F32),
         vm((NX, 16, E), F32), vm((NX - 1, 16, E), F32), vm((3, 16, E), F32),
         vm((NY - 1, 16, E), F32), vm((NZ - 1, 16, E), F32),
@@ -601,9 +631,9 @@
     scratch += [dma((4,)), dma((1,)), dma((1,))]
     scratch += [dma((STEPS,))] * 4
     scratch += [dma((STEPS, 4))] * 2
-    scratch += [dma((NX,))] * 2
-    scratch += [dma((NX, NY))] * 2
-    scratch += [dma((NX,))] * 4
+    scratch += [dma((NX, 2))] * 2
+    scratch += [dma((NX, NY, 2))] * 2
+    scratch += [dma((NX, 2))] * 4
     scratch += [dma((NZ,))] * 2
     scratch += [dma] * 2
     scratch += [dma((8,))] * 6

time: 103 us -> 102 us (level)
    pallas_call x1, Pallas kernels: 98.8 us -> 97.8 us  [local(): pl.pallas_call(kernel, out_shape=(jax.ShapeDtypeStruct((ROWS, E), F32), j...]
where the time goes in v5:
time: 102 us
  Pallas kernels  101 us (99%)
    pallas_call x1, Pallas kernels, local(): pl.pallas_call(kernel, out_shape=(jax.ShapeDtypeStruct((ROWS, E), F32), j...  97.8 us
    pallas_call x1, Pallas kernels, local(): pl.pallas_call(finish, out_shape=(jax.ShapeDtypeStruct((ROWS, E), F32), j...  3.1 us

profile of v5, /device:TPU:32, one launch (start us, length us, event | category | flops | bytes accessed | tf_op | source)
XLA Modules:
  0.0 101.5 jit_solution(6724027145663502696)
XLA Ops:
  0.6 97.8 %shard_map.136 = (f32[2048,128]{1,0:T(8,128)}, f32[16,128]{1,0:T(8,128)}, f32[16,512]{1,0:T(8,128)}, f32[8,128]{1,0:T(8,128)}) custom-call(f32[2048,128]{1,0:T(8,128)} %table_in.1, f32[16,128]{1,0:T(8,128)} %bitcast.15, s32[3,4,64]{2,1,0:T(4,128)} %bitcast.17, s32[3,104,128]{2,1,0:T(8,128)} %bitcast.13, s32[3,128]{1,0:T(4,128)} %labels.1, ...), custom_call_target="tpu_custom_call" | custom-call | tf_op jit(solution)/shard_map/pallas_call | solution.py:642
  98.4 3.1 %shard_map.137 = (f32[2048,128]{1,0:T(8,128)}, f32[16,128]{1,0:T(8,128)}, f32[13,256]{1,0:T(8,128)}, f32[13,256]{1,0:T(8,128)}, f32[1,13]{1,0:T(1,128)}, /*index=5*/f32[1,13]{1,0:T(1,128)}) custom-call(f32[2048,128]{1,0:T(8,128)} %get-tuple-element.16.table_in, f32[16,128]{1,0:T(8,128)} %get-tuple-element.17.accum_in, f32[16,512]{1,0:T(8,128)} %get-tuple-element.18.gdu, ...), custom_call_target="tpu_custom_call" | custom-call | tf_op jit(solution)/shard_map/pallas_call | solution.py:660

commit v6 on v5

--- a/solution.py
+++ b/solution.py
@@ -75,7 +75,7 @@
     table_in, accum_in, reqs, mem_in, labels, down_in, up_in, bias, outw,
     table_hbm, accum_out, gdu_out, bo_out,
     table, mem, down, up,
-    rqs, rqr, wcol, wrow, s1, r1, g1, g2, rr, rt,
+    rqs, rqr, acc_q, base_q, same, match, back, wcol, wrow, s1, r1, g1, g2, rr, rt,
     rpad, outf, both_t, up_t, bias_b, out_b, acc_b, posq,
     counts, x0s, glows, dlows, us, x1s, heads,
     xw, xo, glowp, dlowp, sa, ra, sb, rb, a2, ra2, b2, rb2, z3, rz,
@@ -241,6 +241,62 @@
     for j in range(NROW):
         rows = rows + nn(rr[j], table[j * CH:(j + 1) * CH, :].astype(BF16))
     put(s1, 0, rows)
+
+    def halves(v):
+        hi = v.astype(BF16)
+        return jnp.concatenate([hi, (v - hi.astype(F32)).astype(BF16)], axis=1)
+
+    def update_all():
+        def chunk(j, carry):
+            at = al(j * CH, CH)
+            rg = nn(rt[j], back[...])
+            rg = rg[:, :E] + rg[:, E:]
+            acc = acc_b[pl.ds(at, CH), :] + jnp.mean(rg * rg, axis=1, keepdims=True)
+            acc_b[pl.ds(at, CH), :] = acc
+            table[pl.ds(at, CH), :] = table[pl.ds(at, CH), :] - learn_rate * rg * lax.rsqrt(acc)
+            return carry
+
+        lax.fori_loop(0, NROW, chunk, 0, unroll=UNROLL_ROWS)
+
+    def exact_rows(src):
+        def chunk(j, total):
+            v = src[pl.ds(al(j * CH, CH), CH), :]
+            hi = v.astype(BF16)
+            rest = v - hi.astype(F32)
+            mid = rest.astype(BF16)
+            lo = (rest - mid.astype(F32)).astype(BF16)
+            return total + nn(rr[j], jnp.concatenate([hi, mid, lo], axis=1))
+
+        total = lax.fori_loop(0, NROW, chunk, jnp.zeros((FETCH, 3 * E), F32), unroll=UNROLL_ROWS)
+        return total[:, :E] + total[:, E:2 * E] + total[:, 2 * E:]
+
+    def prepare(t):
+        lane = iota((CH, E), 1)
+
+        def chunk(j, total):
+            v = acc_b[pl.ds(al(j * CH, CH), CH), :]
+            hi = v.astype(BF16).astype(F32)
+            mid = (v - hi).astype(BF16).astype(F32)
+            part = jnp.where(lane == 0, hi, jnp.where(lane == 1, mid, v - hi - mid))
+            return total + nn(rr[j], part.astype(BF16))
+
+        total = lax.fori_loop(0, NROW, chunk, jnp.zeros((FETCH, E), F32), unroll=UNROLL_ROWS)
+        total = total[:, 0:1] + total[:, 1:2] + total[:, 2:3]
+        acc_q[...] = jnp.broadcast_to(total, (FETCH, E))
+        pick(t + 1)
+        base_q[...] = exact_rows(table)
+
+    def pair_up(t):
+        row = wrow[t][0:1, :]
+
+        def equal(col, row):
+            return jnp.concatenate([onehot(col == row[:, :E]), onehot(col == row[:, E:])], axis=1)
+
+        alike = equal(wcol[t], row)
+        same[...] = alike
+        earlier = onehot(iota((FETCH, FETCH), 0) < iota((FETCH, FETCH), 1))
+        seen = nn(jnp.ones((16, FETCH), BF16), alike * earlier)[0:1, :]
+        match[...] = equal(wcol[t + 1], jnp.where(seen > 0.5, -1, row))
 
     def copy_to(src, dst, send, recv, peer):
         return pltpu.make_async_remote_copy(
@@ -375,7 +431,6 @@
         for k in range(1, NY):
             bo_y(k).start()
         first(0)
-        first(1)
 
     def first(h):
         for k in range(1, NX):
@@ -426,8 +481,17 @@
     def step(t, carry):
         send_all(s1.at[t], r1.at[t], s1s.at[t], s1r.at[t])
         r1[t, owner] = s1[t, owner]
+
+        @pl.when(t > 0)
+        def _():
+            update_all()
+
         place(t)
-        pick(jnp.minimum(t + 1, STEPS - 1))
+
+        @pl.when(t < STEPS - 1)
+        def _():
+            prepare(t)
+
         cur = lax.rem(t, 2)
         sent_all(s1.at[t], r1.at[t], s1s.at[t], s1r.at[t]).wait_recv()
         fetched_t = nt(eye_e, take(r1, t).astype(BF16)).astype(BF16)
@@ -489,6 +553,7 @@
 
         @pl.when(t < STEPS - 1)
         def _():
+            pair_up(t)
             count(t + 1)
             windows(t)
 
@@ -498,28 +563,22 @@
             sums()
 
         sent_all(g1.at[t], g2.at[t], g1s.at[t], g1r.at[t]).wait_recv()
-        back = take(g2, t)
-        hi = back.astype(BF16)
-        pair = jnp.concatenate([hi, (back - hi.astype(F32)).astype(BF16)], axis=1)
-
-        def update(j, carry):
-            at = al(j * CH, CH)
-            rg = nn(rt[j], pair)
+        pair = halves(take(g2, t))
+        back[...] = pair
+
+        @pl.when(t < STEPS - 1)
+        def _():
+            rg = nn(same[...], pair)
             rg = rg[:, :E] + rg[:, E:]
-            acc = acc_b[pl.ds(at, CH), :] + jnp.mean(rg * rg, axis=1, keepdims=True)
-            acc_b[pl.ds(at, CH), :] = acc
-            table[pl.ds(at, CH), :] = table[pl.ds(at, CH), :] - learn_rate * rg * lax.rsqrt(acc)
-            return carry
-
-        def gather(j, rows):
-            return rows + nn(rr[j], table[pl.ds(al(j * CH, CH), CH), :].astype(BF16))
-
-        lax.fori_loop(0, NROW, update, 0, unroll=UNROLL_ROWS)
-        rows = lax.fori_loop(0, NROW, gather, jnp.zeros((FETCH, E), F32), unroll=NROW)
-        put(s1, t + 1, rows)
+            acc = acc_q[...] + jnp.mean(rg * rg, axis=1, keepdims=True)
+            moved = nn(match[...], halves(learn_rate * rg * lax.rsqrt(acc)))
+            put(s1, t + 1, base_q[...] - (moved[:, :E] + moved[:, E:]))
+
         return carry
 
     lax.fori_loop(0, STEPS, step, 0)
+    second()
+    update_all()
 
     store = pltpu.make_async_copy(table, table_hbm, lsem.at[0])
     store.start()
@@ -531,7 +590,7 @@
 
     lax.fori_loop(0, ROWS // E, acc_rows, 0)
 
-    second()
+    first(1)
     for k in range(1, NY):
         bo_y(k).wait()
     bv[1] = bv[0] + bvy[0] + bvy[1] + bvy[2]
@@ -605,6 +664,8 @@
         vm((ROWS, E), F32), vm((STEPS, NB * BAGLEN, TOK), jnp.int32),
         vm((D_IN, RANK), BF16), vm((RANK, D_IN), BF16),
         vm((OWNERS, 1, E), F32), vm((OWNERS, 1, E), F32),
+        vm((FETCH, E), F32), vm((FETCH, E), F32),
+        vm((FETCH, FETCH), BF16), vm((FETCH, FETCH), BF16), vm((FETCH, 2 * E), BF16),
         vm((STEPS, FETCH, E), jnp.int32), vm((STEPS, 8, FETCH), jnp.int32),
         vm((STEPS + 1, OWNERS, SLOTS, E), F32),
     ]

time: 102 us -> 102 us (level)
  no operation moved by 1% of the time
where the time goes in v6:
time: 102 us; the launch traced here: 101 us
  Pallas kernels  101 us (99%)
    pallas_call x1, Pallas kernels, local(): pl.pallas_call(kernel, out_shape=(jax.ShapeDtypeStruct((ROWS, E), F32), j...  97.5 us
    pallas_call x1, Pallas kernels, local(): pl.pallas_call(finish, out_shape=(jax.ShapeDtypeStruct((ROWS, E), F32), j...  3.1 us

profile of v6, /device:TPU:32, one launch (start us, length us, event | category | flops | bytes accessed | tf_op | source)
XLA Modules:
  0.0 101.3 jit_solution(3222107403314827433)
XLA Ops:
  0.6 97.5 %shard_map.136 = (f32[2048,128]{1,0:T(8,128)}, f32[16,128]{1,0:T(8,128)}, f32[16,512]{1,0:T(8,128)}, f32[8,128]{1,0:T(8,128)}) custom-call(f32[2048,128]{1,0:T(8,128)} %table_in.1, f32[16,128]{1,0:T(8,128)} %bitcast.15, s32[3,4,64]{2,1,0:T(4,128)} %bitcast.17, s32[3,104,128]{2,1,0:T(8,128)} %bitcast.13, s32[3,128]{1,0:T(4,128)} %labels.1, ...), custom_call_target="tpu_custom_call" | custom-call | tf_op jit(solution)/shard_map/pallas_call | solution.py:703
  98.2 3.1 %shard_map.137 = (f32[2048,128]{1,0:T(8,128)}, f32[16,128]{1,0:T(8,128)}, f32[13,256]{1,0:T(8,128)}, f32[13,256]{1,0:T(8,128)}, f32[1,13]{1,0:T(1,128)}, /*index=5*/f32[1,13]{1,0:T(1,128)}) custom-call(f32[2048,128]{1,0:T(8,128)} %get-tuple-element.16.table_in, f32[16,128]{1,0:T(8,128)} %get-tuple-element.17.accum_in, f32[16,512]{1,0:T(8,128)} %get-tuple-element.18.gdu, ...), custom_call_target="tpu_custom_call" | custom-call | tf_op jit(solution)/shard_map/pallas_call | solution.py:721

commit v7 on v6

--- a/solution.py
+++ b/solution.py
@@ -176,7 +176,7 @@
             counts[lax.rem(t, 2), i] = jnp.concatenate(cnt, axis=1)
             return carry
 
-        lax.fori_loop(0, NCH, bags, 0)
+        lax.fori_loop(0, NCH, bags, 0, unroll=UNROLL)
 
     loads[0].wait()
     loads[1].wait()
@@ -190,7 +190,7 @@
         both_t[RANK:, pl.ds(at, CH)] = (up_c.astype(F32) * w_row).astype(BF16)
         return carry
 
-    lax.fori_loop(0, NCH, weights, 0)
+    lax.fori_loop(0, NCH, weights, 0, unroll=UNROLL)
 
     def acc_columns(i, carry):
         at = al(i * E, E)
@@ -219,14 +219,14 @@
             rr[j] = jnp.concatenate([onehot(want == lanes), onehot(want == lanes + E)], axis=1)
             return carry
 
-        lax.fori_loop(0, NROW, chunk, 0)
+        lax.fori_loop(0, NROW, chunk, 0, unroll=NROW)
 
     def place(t):
         def chunk(j, carry):
             rt[j] = onehot(iota((CH, FETCH), 0) + j * CH == wrow[t][0:1, :])
             return carry
 
-        lax.fori_loop(0, NROW, chunk, 0)
+        lax.fori_loop(0, NROW, chunk, 0, unroll=NROW)
 
     def put(dst, t, rows):
         for s in range(SLOTS):
@@ -513,10 +513,6 @@
         v = total[RANK:]
         vb = v.astype(BF16)
 
-        @pl.when(t == STEPS - 1)
-        def _():
-            windows(t)
-
         def forward(i, logit):
             at = al(i * CH, CH)
             gate = nn(up_t[pl.ds(at, CH), :], low) + bias_b[pl.ds(at, CH), :]
@@ -540,6 +536,11 @@
         glows[t] = (dlogit * low.astype(F32)).astype(BF16)
         dlow_copy(t).start()
         glow_copy(t).start()
+
+        @pl.when(t == STEPS - 1)
+        def _():
+            windows(t)
+
 
         def spread(i, gf):
             at = al(i * CH, CH)

time: 102 us -> 100 us (0.980)
  Pallas kernels: 101 us -> 99.4 us
    pallas_call x1, Pallas kernels: 97.5 us -> 96.3 us  [local(): pl.pallas_call(kernel, out_shape=(jax.ShapeDtypeStruct((ROWS, E), F32), j...]
where the time goes in v7:
time: 100 us
  Pallas kernels  99.4 us (99%)
    pallas_call x1, Pallas kernels, local(): pl.pallas_call(kernel, out_shape=(jax.ShapeDtypeStruct((ROWS, E), F32), j...  96.3 us
    pallas_call x1, Pallas kernels, local(): pl.pallas_call(finish, out_shape=(jax.ShapeDtypeStruct((ROWS, E), F32), j...  3.1 us

profile of v7, /device:TPU:32, one launch (start us, length us, event | category | flops | bytes accessed | tf_op | source)
XLA Modules:
  0.0 100.2 jit_solution(15332901812143350659)
XLA Ops:
  0.6 96.3 %shard_map.136 = (f32[2048,128]{1,0:T(8,128)}, f32[16,128]{1,0:T(8,128)}, f32[16,512]{1,0:T(8,128)}, f32[8,128]{1,0:T(8,128)}) custom-call(f32[2048,128]{1,0:T(8,128)} %table_in.1, f32[16,128]{1,0:T(8,128)} %bitcast.15, s32[3,4,64]{2,1,0:T(4,128)} %bitcast.17, s32[3,104,128]{2,1,0:T(8,128)} %bitcast.13, s32[3,128]{1,0:T(4,128)} %labels.1, ...), custom_call_target="tpu_custom_call" | custom-call | tf_op jit(solution)/shard_map/pallas_call | solution.py:704
  97.0 3.1 %shard_map.137 = (f32[2048,128]{1,0:T(8,128)}, f32[16,128]{1,0:T(8,128)}, f32[13,256]{1,0:T(8,128)}, f32[13,256]{1,0:T(8,128)}, f32[1,13]{1,0:T(1,128)}, /*index=5*/f32[1,13]{1,0:T(1,128)}) custom-call(f32[2048,128]{1,0:T(8,128)} %get-tuple-element.16.table_in, f32[16,128]{1,0:T(8,128)} %get-tuple-element.17.accum_in, f32[16,512]{1,0:T(8,128)} %get-tuple-element.18.gdu, ...), custom_call_target="tpu_custom_call" | custom-call | tf_op jit(solution)/shard_map/pallas_call | solution.py:722
